TPU v7x, 128 devices: a whole 4x4x4 slice. The times are simulated.
128 devices in a mesh: seq: 32 (over y, x, core), tp: 4 (over z).
Axes of the slice: x: 4, y: 4, z: 4, core: 2. Of those that a mesh axis runs over, the one named last changes fastest.
Arguments:
- seg_tokens: bfloat16 [32768, 3, 4096], P('seq', None, 'tp'), may hold values from -6 to 6
- seg_length: int32 [32], P('seq'), may hold values from 0 to 1024, as said below
- seg_offset: int32 [32], P('seq'), may hold values from 0 to 16128, as said below
- short_weight: float32 [3, 3, 4096], P(None, None, 'tp'), may hold values from -3.5 to 3.5
- residues: float32 [16, 4096], P(None, 'tp'), may hold values from -4 to 4
- filter_span: float32 [16, 4096], P(None, 'tp'), may hold values from 30 to 65536
- skip_gain: float32 [4096], P('tp'), may hold values from -4 to 4
- out_weight: bfloat16 [4096, 4096], P('tp'), may hold values from -0.09375 to 0.09375
Outputs:
- mixed: bfloat16 [16384, 4096], P(('seq', 'tp'))
Inputs may be any that keep to these rules, and one draw needn't show every extreme that they name: Segment s has seg_length[s] valid rows at the head of its buffer; the segments laid end to end in order cover the 16384 positions exactly, and each segment's first and last position lie within 256 positions of s * 512 and (s + 1) * 512 - 1. seg_offset[s] is the sum of seg_length over the segments before s.
All inputs are finite; a program needn't handle non-finite values.
Results may differ from a plain program's by a relative error of at most 0.02.
Values may be sent and summed in bfloat16 or wider, within the bound.
A program may use at most 128 MiB of HBM per device.

v0:
```python
import math

import jax
import jax.numpy as jnp
from jax import lax
from jax.sharding import PartitionSpec as P

TWO_PI = 2.0 * math.pi
HIGHEST = lax.Precision.HIGHEST


def with_halo(cells, sides, width):
    for axis, dim in sides:
        count = lax.axis_size(axis)
        ends = count - 1
        head = lax.slice_in_dim(cells, 0, width, axis=dim)
        tail = lax.slice_in_dim(cells, cells.shape[dim] - width, cells.shape[dim], axis=dim)
        cells = jnp.concatenate(
            [
                lax.ppermute(tail, axis, [(i, (i + 1) % count) for i in range(ends)]),
                cells,
                lax.ppermute(head, axis, [((i + 1) % count, i) for i in range(ends)]),
            ],
            axis=dim,
        )
    return cells


def angle_table(row_count, col_count, period, row_first, col_first):
    row_ids = row_first + lax.iota(jnp.int32, row_count)
    col_ids = col_first + lax.iota(jnp.int32, col_count)
    product = row_ids[:, None] * col_ids[None, :] % period
    angles = product.astype(jnp.float32) * (TWO_PI / period)
    return (jnp.cos(angles), jnp.sin(angles))


def contract(formula, left, right):
    return jnp.einsum(formula, left, right, precision=HIGHEST, preferred_element_type=jnp.float32)


def filter_spectrum(freq, weights, spans, total):
    theta = freq.astype(jnp.float32) * (TWO_PI / total)
    parity = (1 - 2 * (freq % 2)).astype(jnp.float32)
    half_sine = jnp.sin(0.5 * theta)
    sine = jnp.sin(theta)
    spec_real = jnp.zeros((), jnp.float32)
    spec_imag = jnp.zeros((), jnp.float32)
    for order_id in range(weights.shape[0]):
        rate = 1.0 / spans[order_id]
        decay = jnp.exp(-rate)
        denom_real = -jnp.expm1(-rate) + 2.0 * decay * half_sine * half_sine
        denom_imag = decay * sine
        numer = 1.0 - parity * jnp.exp(-rate * float(total // 2))
        scale = (
            weights[order_id]
            * jnp.sqrt(rate)
            * numer
            / (denom_real * denom_real + denom_imag * denom_imag)
        )
        spec_real = spec_real + scale * denom_real
        spec_imag = spec_imag - scale * denom_imag
    return (spec_real, spec_imag)


def coarse_forward(values, formula, inner_first, inner_count, seq_count, total):
    cos_coarse, sin_coarse = angle_table(2 * seq_count, seq_count, 2 * seq_count, 0, 0)
    part_real = contract(formula, cos_coarse, values)
    part_imag = -contract(formula, sin_coarse, values)
    tw_cos, tw_sin = angle_table(2 * seq_count, inner_count, total, 0, inner_first)
    tw_cos, tw_sin = (tw_cos[:, :, None], tw_sin[:, :, None])
    return (part_real * tw_cos + part_imag * tw_sin, part_imag * tw_cos - part_real * tw_sin)


def fine_filter(
    part_real,
    part_imag,
    formula,
    coarse_first,
    coarse_count,
    rows_here,
    total,
    seq_count,
    weights,
    spans,
):
    cos_fine, sin_fine = angle_table(rows_here, rows_here, rows_here, 0, 0)
    freq_real = contract(formula, part_real, cos_fine) + contract(formula, part_imag, sin_fine)
    freq_imag = contract(formula, part_imag, cos_fine) - contract(formula, part_real, sin_fine)
    coarse_ids = coarse_first + lax.iota(jnp.int32, coarse_count)
    freq = coarse_ids[:, None] + 2 * seq_count * lax.iota(jnp.int32, rows_here)[None, :]
    tw_cos, tw_sin = angle_table(coarse_count, rows_here, total, coarse_first, 0)
    freq = freq[:, :, None]
    tw_cos, tw_sin = (tw_cos[:, :, None], tw_sin[:, :, None])
    spec_real, spec_imag = filter_spectrum(freq, weights, spans, total)
    prod_real = freq_real * spec_real - freq_imag * spec_imag
    prod_imag = freq_real * spec_imag + freq_imag * spec_real
    back_real = contract(formula, prod_real, cos_fine) - contract(formula, prod_imag, sin_fine)
    back_imag = contract(formula, prod_imag, cos_fine) + contract(formula, prod_real, sin_fine)
    return (back_real * tw_cos - back_imag * tw_sin, back_imag * tw_cos + back_real * tw_sin)


def coarse_inverse(back_real, back_imag, formula, seq_count, total):
    cos_coarse, sin_coarse = angle_table(seq_count, 2 * seq_count, 2 * seq_count, 0, 0)
    summed = contract(formula, cos_coarse, back_real) - contract(formula, sin_coarse, back_imag)
    return summed / float(total)


def shards(
    seg_tokens, seg_length, seg_offset, short_weight, residues, filter_span, skip_gain, out_weight
):
    buffer_rows = seg_tokens.shape[0]
    rows_here = buffer_rows // 2
    channels = seg_tokens.shape[2]
    seq_count = lax.axis_size("seq")
    seq_index = lax.axis_index("seq")
    total = 2 * rows_here * seq_count
    lag_rows = short_weight.shape[0] - 1
    rim_rows = rows_here // 2 + 8
    seg_len = seg_length[0]
    seg_start = seg_offset[0]
    head_rows = seg_tokens[:rim_rows]
    tail_ids = seg_len - rim_rows + lax.iota(jnp.int32, rim_rows)
    tail_rows = jnp.take(seg_tokens, jnp.clip(tail_ids, 0, buffer_rows - 1), axis=0)
    tail_rows = jnp.where((tail_ids >= 0)[:, None, None], tail_rows, jnp.zeros_like(tail_rows))
    edges = jnp.concatenate([head_rows, tail_rows], axis=0)
    extended = with_halo(edges, (("seq", 0),), rim_rows)
    pool = jnp.concatenate([extended[:rim_rows], seg_tokens, extended[3 * rim_rows :]], axis=0)
    wanted = seq_index * rows_here - lag_rows + lax.iota(jnp.int32, rows_here + lag_rows)
    relative = wanted - seg_start
    pool_ids = jnp.where(
        relative < 0,
        relative + rim_rows,
        jnp.where(
            relative < seg_len, rim_rows + relative, rim_rows + buffer_rows + relative - seg_len
        ),
    )
    picked = jnp.take(pool, pool_ids, axis=0).astype(jnp.float32)
    features = jnp.zeros((rows_here, 3, channels), jnp.float32)
    for shift_id in range(lag_rows + 1):
        features = (
            features
            + short_weight[shift_id] * picked[lag_rows - shift_id : lag_rows - shift_id + rows_here]
        )
    gated = (features[:, 1, :] * features[:, 2, :]).astype(jnp.bfloat16)
    block_rows = rows_here // seq_count
    regrouped = lax.all_to_all(
        gated.reshape(1, rows_here, channels), "seq", split_axis=1, concat_axis=0, tiled=True
    )
    part_real, part_imag = coarse_forward(
        regrouped.astype(jnp.float32),
        "kn,nbc->kbc",
        seq_index * block_rows,
        block_rows,
        seq_count,
        total,
    )
    part_real, part_imag = (
        lax.all_to_all(
            part_real.astype(jnp.bfloat16), "seq", split_axis=0, concat_axis=1, tiled=True
        ).astype(part_real.dtype),
        lax.all_to_all(
            part_imag.astype(jnp.bfloat16), "seq", split_axis=0, concat_axis=1, tiled=True
        ).astype(part_imag.dtype),
    )
    back_real, back_imag = fine_filter(
        part_real,
        part_imag,
        "amc,mk->akc",
        2 * seq_index,
        2,
        rows_here,
        total,
        seq_count,
        residues[:, None, None, :],
        filter_span[:, None, None, :],
    )
    back_real, back_imag = (
        lax.all_to_all(
            back_real.astype(jnp.bfloat16), "seq", split_axis=1, concat_axis=0, tiled=True
        ).astype(back_real.dtype),
        lax.all_to_all(
            back_imag.astype(jnp.bfloat16), "seq", split_axis=1, concat_axis=0, tiled=True
        ).astype(back_imag.dtype),
    )
    pieces = coarse_inverse(back_real, back_imag, "nk,kbc->nbc", seq_count, total)
    conv = (
        lax.all_to_all(pieces.astype(jnp.bfloat16), "seq", split_axis=0, concat_axis=1, tiled=True)
        .astype(pieces.dtype)
        .reshape(rows_here, channels)
    )
    mixer = (features[:, 0, :] * (conv + skip_gain * gated.astype(jnp.float32))).astype(
        jnp.bfloat16
    )
    return lax.psum_scatter(
        jnp.dot(mixer, out_weight, preferred_element_type=jnp.float32).astype(jnp.bfloat16),
        "tp",
        scatter_dimension=0,
        tiled=True,
    )


def solution(mesh):
    in_specs = (
        P("seq", None, "tp"),
        P("seq"),
        P("seq"),
        P(None, None, "tp"),
        P(None, "tp"),
        P(None, "tp"),
        P("tp"),
        P("tp", None),
    )
    out_specs = P(("seq", "tp"), None)
    return jax.shard_map(shards, mesh=mesh, in_specs=in_specs, out_specs=out_specs, check_vma=False)
```

profile of v0, /device:TPU:1, one launch (start us, length us, event | category | flops | bytes accessed | tf_op | source)
XLA Modules:
  0.0 557.4 jit_solution(8504752020750377586)
XLA Ops:
  12.1 14.7 %gather_fusion = bf16[264,3,1024]{2,0,1:T(8,128)(2,1)S(1)} fusion(bf16[1024,3,1024]{2,0,1:T(8,128)(2,1)} %param.8, s32[1024]{0:T(1024)S(1)} %pad_clamp_fusion.1), kind=kCustom, calls=%fused_computation | custom fusion | bytes 3245088 | tf_op jit(solution)/shard_map/jit(_take)/gather | solution.py:123
  33.0 11.4 %copy.36 = bf16[1024,3,1024]{2,1,0:T(4,128)(2,1)} copy(bf16[1024,3,1024]{2,0,1:T(8,128)(2,1)} %param.8) | data formatting | bytes 12582912 | tf_op args[0]
  51.0 41.5 %pad_maximum_fusion = bf16[1552,3,1024]{2,1,0:T(4,128)(2,1)} fusion(bf16[264,3,1024]{2,1,0:T(4,128)(2,1)S(1)} %copy.37, bf16[1024,3,1024]{2,1,0:T(4,128)(2,1)} %copy.36, bf16[264,3,1024]{2,1,0:T(4,128)(2,1)S(1)} %copy.35), kind=kLoop, calls=%fused_computation.2 | loop fusion | flops 9535488 | bytes 19070976 | tf_op jit(solution)/shard_map/concatenate | solution.py:127
  92.4 27.2 %gather_fusion.1 = bf16[514,3,1024]{2,1,0:T(4,128)(2,1)} fusion(bf16[1552,3,1024]{2,1,0:T(4,128)(2,1)} %pad_maximum_fusion, s32[1024]{0:T(1024)S(1)} %pad_clamp_fusion), kind=kCustom, calls=%fused_computation.1 | custom fusion | bytes 6318088 | tf_op jit(solution)/shard_map/jit(_take)/gather | solution.py:137
  119.7 4.6 select_convert_fusion
  124.2 6.6 %fusion = f32[512,3,1024]{2,1,0:T(4,128)S(1)} fusion(f32[514,3,1024]{2,1,0:T(4,128)S(1)} %select_convert_fusion, f32[3,1024]{1,0:T(4,128)S(1)} %get-tuple-element.76, f32[3,1024]{1,0:T(4,128)S(1)} %get-tuple-element.77, f32[3,1024]{1,0:T(4,128)S(1)} %get-tuple-element.75), kind=kLoop, calls=%fused_computation.4 | loop fusion | flops 7864320 | bytes 25202688 | tf_op jit(solution)/shard_map/add | solution.py:141
  130.9 6.0 %fusion.194 = (f32[512,1,1024]{2,1,0:T(1,128)}, bf16[512,1,1024]{2,1,0:T(2,128)(2,1)S(1)}, f32[512,1,1024]{2,1,0:T(1,128)}) fusion(f32[512,3,1024]{2,1,0:T(4,128)S(1)} %fusion), kind=kLoop, calls=%fused_computation.393 | loop fusion | flops 1572864 | bytes 11534336 | tf_op jit(solution)/shard_map/convert_element_type | solution.py:191
  139.6 6.8 %reduce.4 = bf16[512,1024]{1,0:T(8,128)(2,1)S(1)} reduce(bf16[512,1,1024]{2,1,0:T(2,128)(2,1)S(1)} %bitcast_bitcast_fusion, bf16[]{:T(256)} %broadcast.1128), dimensions={1}, to_apply=%bitcast_bitcast_fusion.reduce_sub_computation | reduce | bytes 2097154
  147.9 16.1 %all-to-all-start = ((bf16[32,2,8192]{2,1,0:T(2,128)(2,1)}), bf16[32,2,8192]{2,1,0:T(2,128)(2,1)S(1)}, u32[]{:S(2)}, u32[]{:S(2)}) async-start(bf16[32,2,8192]{2,1,0:T(2,128)(2,1)} %reshape.1282), calls=%async_computation | async-start | bytes 2097152 | tf_op jit(solution)/shard_map/all_to_all | solution.py:146
  164.3 16.8 %all-to-all-done = bf16[32,2,8192]{2,1,0:T(2,128)(2,1)S(1)} async-done(((bf16[32,2,8192]{2,1,0:T(2,128)(2,1)}), bf16[32,2,8192]{2,1,0:T(2,128)(2,1)S(1)}, u32[]{:S(2)}, u32[]{:S(2)}) %all-to-all-start) | async-done | bytes 1048608 | tf_op jit(solution)/shard_map/all_to_all | solution.py:146
  185.2 5.1 add_convert_fusion
  201.4 23.4 %all-to-all-done.1 = bf16[64,16,1024]{2,1,0:T(8,128)(2,1)S(1)} async-done(((bf16[64,16,1024]{2,1,0:T(8,128)(2,1)}), bf16[64,16,1024]{2,1,0:T(8,128)(2,1)S(1)}, u32[]{:S(2)}, u32[]{:S(2)}) %all-to-all-start.1) | async-done | bytes 2097184 | tf_op jit(solution)/shard_map/all_to_all | solution.py:158
  224.8 7.1 %all-to-all-start.2 = ((bf16[64,16,1024]{2,1,0:T(8,128)(2,1)}), bf16[64,16,1024]{2,1,0:T(8,128)(2,1)}, u32[]{:S(2)}, u32[]{:S(2)}) async-start(bf16[64,16,1024]{2,1,0:T(8,128)(2,1)} %copy.44), calls=%async_computation.2 | async-start | bytes 4194304 | tf_op jit(solution)/shard_map/all_to_all | solution.py:161
  238.4 21.2 %all-to-all-done.2 = bf16[64,16,1024]{2,1,0:T(8,128)(2,1)} async-done(((bf16[64,16,1024]{2,1,0:T(8,128)(2,1)}), bf16[64,16,1024]{2,1,0:T(8,128)(2,1)}, u32[]{:S(2)}, u32[]{:S(2)}) %all-to-all-start.2) | async-done | bytes 2097184 | tf_op jit(solution)/shard_map/all_to_all | solution.py:161
  261.3 7.3 %fusion.72 = f32[512,2,1024]{2,0,1:T(8,128)S(1)} fusion(bf16[2,512,1024]{2,1,0:T(8,128)(2,1)S(1)} %bitcast.207), kind=kOutput, calls=%fused_computation.152 | convolution fusion | flops 6446120960 | bytes 6291456 | tf_op jit(solution)/shard_map/amc,mk->akc/dot_general | solution.py:38
  268.7 7.5 %fusion.74 = f32[512,2,1024]{2,0,1:T(8,128)S(1)} fusion(bf16[2,512,1024]{2,1,0:T(8,128)(2,1)S(1)} %bitcast.214), kind=kOutput, calls=%fused_computation.154 | convolution fusion | flops 6446120960 | bytes 6291456 | tf_op jit(solution)/shard_map/amc,mk->akc/dot_general | solution.py:38
  276.2 7.4 %convolution_add_fusion = f32[512,2,1024]{2,0,1:T(8,128)S(1)} fusion(f32[512,2,1024]{2,0,1:T(8,128)S(1)} %fusion.74, bf16[2,512,1024]{2,1,0:T(8,128)(2,1)S(1)} %bitcast.208), kind=kOutput, calls=%fused_computation.124 | convolution fusion | flops 6447169536 | bytes 10485760 | tf_op jit(solution)/shard_map/amc,mk->akc/dot_general | solution.py:38
  283.7 49.7 %fusion.54 = (f32[2,512,1024]{2,1,0:T(8,128)S(1)}, f32[2,512,1024]{2,1,0:T(8,128)}, f32[2,512,1024]{2,1,0:T(8,128)}, f32[512,2,1024]{2,0,1:T(8,128)}) fusion(f32[512,2,1024]{2,0,1:T(8,128)S(1)} %convolution_add_fusion, f32[1024]{0:T(1024)S(1)} %bitcast.230, f32[1024]{0:T(1024)S(1)} %broadcast_multiply_fusion, f32[1024]{0:T(1024)S(1)} %bitcast.278, ...), kind=kOutput, calls=%fused_computation.100 | convolution fusion | flops 6697254912 | bytes 28651520 | tf_op jit(solution)/shard_map/amc,mk->akc/dot_general | solution.py:38
  333.5 6.7 %fusion.55 = f32[2,512,1024]{2,1,0:T(8,128)S(1)} fusion(f32[2,512,1024]{2,1,0:T(8,128)} %get-tuple-element.7, f32[512,2,1024]{2,0,1:T(8,128)} %get-tuple-element.134, f32[2,512,1024]{2,1,0:T(8,128)} %get-tuple-element.6, f32[512,2,1024]{2,0,1:T(8,128)S(1)} %convolution_add_fusion), kind=kLoop, calls=%fused_computation.101 | loop fusion | flops 3145728 | bytes 20971520 | tf_op jit(solution)/shard_map/add | solution.py:96
  340.2 10.8 %fusion.68 = f32[512,2,1024]{2,0,1:T(8,128)S(1)} fusion(f32[2,512,1024]{2,1,0:T(8,128)S(1)} %fusion.55), kind=kOutput, calls=%fused_computation.148 | convolution fusion | flops 6446120960 | bytes 8388608 | tf_op jit(solution)/shard_map/amc,mk->akc/dot_general | solution.py:38
  351.0 10.6 %fusion.70 = f32[512,2,1024]{2,0,1:T(8,128)S(1)} fusion(f32[2,512,1024]{2,1,0:T(8,128)S(1)} %get-tuple-element.5), kind=kOutput, calls=%fused_computation.150 | convolution fusion | flops 6446120960 | bytes 8388608 | tf_op jit(solution)/shard_map/amc,mk->akc/dot_general | solution.py:38
  361.6 11.4 %convolution_subtract_fusion.1 = f32[512,2,1024]{2,0,1:T(8,128)S(1)} fusion(f32[512,2,1024]{2,0,1:T(8,128)S(1)} %fusion.70, f32[2,512,1024]{2,1,0:T(8,128)S(1)} %fusion.55), kind=kOutput, calls=%fused_computation.126 | convolution fusion | flops 6447169536 | bytes 12582912 | tf_op jit(solution)/shard_map/amc,mk->akc/dot_general | solution.py:38
  373.0 13.8 %fusion.53 = (bf16[2,512,1024]{2,1,0:T(8,128)(2,1)S(1)}, bf16[2,512,1024]{2,1,0:T(8,128)(2,1)}) fusion(f32[512,2,1024]{2,0,1:T(8,128)S(1)} %convolution_subtract_fusion.1, f32[2,512]{1,0:T(2,128)S(1)} %copy-done.7, f32[2,512]{1,0:T(2,128)S(1)} %copy-done.6, f32[512,2,1024]{2,0,1:T(8,128)S(1)} %fusion.68, f32[2,512,1024]{2,1,0:T(8,128)S(1)} %get-tuple-element.5), kind=kOutput, calls=%fused_computation.95 | convolution fusion | flops 6455558144 | bytes 16785408 | tf_op jit(solution)/shard_map/amc,mk->akc/dot_general | solution.py:38
  390.4 6.1 %all-to-all-start.4 = ((bf16[2,512,1024]{2,0,1:T(2,128)(2,1)}), bf16[2,512,1024]{2,0,1:T(2,128)(2,1)S(1)}, u32[]{:S(2)}, u32[]{:S(2)}) async-start(bf16[2,512,1024]{2,0,1:T(2,128)(2,1)} %copy.48), calls=%async_computation.4 | async-start | bytes 4194304 | tf_op jit(solution)/shard_map/all_to_all | solution.py:181
  396.4 5.1 copy.46
  401.6 22.8 %all-to-all-done.4 = bf16[2,512,1024]{2,0,1:T(2,128)(2,1)S(1)} async-done(((bf16[2,512,1024]{2,0,1:T(2,128)(2,1)}), bf16[2,512,1024]{2,0,1:T(2,128)(2,1)S(1)}, u32[]{:S(2)}, u32[]{:S(2)}) %all-to-all-start.4) | async-done | bytes 2097184 | tf_op jit(solution)/shard_map/all_to_all | solution.py:181
  424.4 6.7 %all-to-all-start.3 = ((bf16[2,512,1024]{2,0,1:T(2,128)(2,1)}), bf16[2,512,1024]{2,0,1:T(2,128)(2,1)}, u32[]{:S(2)}, u32[]{:S(2)}) async-start(bf16[2,512,1024]{2,0,1:T(2,128)(2,1)} %copy.46), calls=%async_computation.3 | async-start | bytes 4194304 | tf_op jit(solution)/shard_map/all_to_all | solution.py:178
  437.6 21.6 %all-to-all-done.3 = bf16[2,512,1024]{2,0,1:T(2,128)(2,1)} async-done(((bf16[2,512,1024]{2,0,1:T(2,128)(2,1)}), bf16[2,512,1024]{2,0,1:T(2,128)(2,1)}, u32[]{:S(2)}, u32[]{:S(2)}) %all-to-all-start.3) | async-done | bytes 2097184 | tf_op jit(solution)/shard_map/all_to_all | solution.py:178
  459.1 4.9 copy.71
  472.6 22.3 %all_to_all.93 = bf16[32,16,1024]{2,1,0:T(8,128)(2,1)S(1)} all-to-all(bf16[32,16,1024]{2,1,0:T(8,128)(2,1)S(1)} %copy.50), channel_id=1, replica_groups=mesh['seq'=32,'tp'=4] {'seq'}, dimensions={0} | all-to-all | bytes 2097152 | tf_op jit(solution)/shard_map/all_to_all | solution.py:187
  495.0 9.7 %convolution_convert_fusion = bf16[512,4096]{1,0:T(8,128)(2,1)} fusion(bf16[1024,4096]{1,0:T(8,128)(2,1)} %param.15, f32[512,1,1024]{2,1,0:T(1,128)S(1)} %copy-done.2, f32[512,1,1024]{2,1,0:T(1,128)S(1)} %copy-done.1, bf16[512,1024]{1,0:T(8,128)(2,1)S(1)} %bitcast.216, f32[1024]{0:T(1024)S(1)} %copy-done.16), kind=kOutput, calls=%fused_computation.40 | convolution fusion | flops 4299685888 | bytes 17829888 | tf_op jit(solution)/shard_map/dot_general | solution.py:195
  504.7 45.6 %reduce-scatter.2.cloned.1.call-done = bf16[128,4096]{1,0:T(8,128)(2,1)} async-done(((bf16[512,4096]{1,0:T(8,128)(2,1)}), bf16[128,4096]{1,0:T(8,128)(2,1)}) %reduce-scatter.2.cloned.1.call-update) | async-done | bytes 1048592 | tf_op jit(solution)/shard_map/reduce_scatter | solution.py:194
  (102 shorter events, 63.2 us)
Async XLA Ops:
  8.1 37.8 %collective-permute-start.1 = (bf16[264,3,1024]{2,0,1:T(8,128)(2,1)S(1)}, bf16[264,3,1024]{2,0,1:T(8,128)(2,1)}, u32[]{:S(2)}, u32[]{:S(2)}) collective-permute-start(bf16[264,3,1024]{2,0,1:T(8,128)(2,1)S(1)} %slice.159), channel_id=1, source_target_pairs={{4,0},{8,4},{12,8},{16,12},{20,16},{24,20},{28,24},{32,28},{36,32}... | collective-permute-start | bytes 4866056 | tf_op jit(solution)/shard_map/ppermute | solution.py:22
  28.3 21.3 %collective-permute-start = (bf16[264,3,1024]{2,0,1:T(8,128)(2,1)}, bf16[264,3,1024]{2,0,1:T(8,128)(2,1)S(1)}, u32[]{:S(2)}, u32[]{:S(2)}) collective-permute-start(bf16[264,3,1024]{2,0,1:T(8,128)(2,1)} %select_select_fusion), channel_id=1, source_target_pairs={{0,4},{4,8},{8,12},{12,16},{16,20},{20,24},{24,28},{28,32},{32,36}... | collective-permute-start | bytes 4866056 | tf_op jit(solution)/shard_map/ppermute | solution.py:20
  33.0 11.4 %copy-start.3 = (f32[16,1024]{1,0:T(8,128)S(1)}, f32[16,1024]{1,0:T(8,128)}, u32[]{:S(2)}) copy-start(f32[16,1024]{1,0:T(8,128)} %param.12) | copy-start | bytes 196612
  33.0 11.4 %copy-start.4 = (f32[16,1024]{1,0:T(8,128)S(1)}, f32[16,1024]{1,0:T(8,128)}, u32[]{:S(2)}) copy-start(f32[16,1024]{1,0:T(8,128)} %param.13) | copy-start | bytes 196612
  33.0 12.8 %copy-start.5 = (f32[3,3,1024]{2,1,0:T(4,128)S(1)}, f32[3,3,1024]{2,1,0:T(4,128)}, u32[]{:S(2)}) copy-start(f32[3,3,1024]{2,1,0:T(4,128)} %param.11) | copy-start | bytes 110596
  147.9 33.2 %all-to-all-start = ((bf16[32,2,8192]{2,1,0:T(2,128)(2,1)}), bf16[32,2,8192]{2,1,0:T(2,128)(2,1)S(1)}, u32[]{:S(2)}, u32[]{:S(2)}) async-start(bf16[32,2,8192]{2,1,0:T(2,128)(2,1)} %reshape.1282), calls=%async_computation | async-start | bytes 2097152 | tf_op jit(solution)/shard_map/all_to_all | solution.py:146
  190.3 6.6 %copy-start.15 = (s32[2]{0:T(128)S(1)}, s32[2]{0:T(128)}, u32[]{:S(2)}) copy-start(s32[2]{0:T(128)} %iota_add_fusion.1) | copy-start | bytes 28
  192.8 32.0 %all-to-all-start.1 = ((bf16[64,16,1024]{2,1,0:T(8,128)(2,1)}), bf16[64,16,1024]{2,1,0:T(8,128)(2,1)S(1)}, u32[]{:S(2)}, u32[]{:S(2)}) async-start(bf16[64,16,1024]{2,1,0:T(8,128)(2,1)} %copy.42), calls=%async_computation.1 | async-start | bytes 4194304 | tf_op jit(solution)/shard_map/all_to_all | solution.py:158
  224.8 34.7 %all-to-all-start.2 = ((bf16[64,16,1024]{2,1,0:T(8,128)(2,1)}), bf16[64,16,1024]{2,1,0:T(8,128)(2,1)}, u32[]{:S(2)}, u32[]{:S(2)}) async-start(bf16[64,16,1024]{2,1,0:T(8,128)(2,1)} %copy.44), calls=%async_computation.2 | async-start | bytes 4194304 | tf_op jit(solution)/shard_map/all_to_all | solution.py:161
  261.3 7.3 %copy-start = (bf16[32,2,16,1024]{3,2,0,1:T(8,128)(2,1)S(1)}, bf16[32,2,16,1024]{3,2,0,1:T(8,128)(2,1)}, u32[]{:S(2)}) copy-start(bf16[32,2,16,1024]{3,2,0,1:T(8,128)(2,1)} %copy.43) | copy-start | bytes 6291460
  276.2 7.5 %copy-start.8 = (f32[1,1024]{1,0:T(1,128)S(1)}, f32[1,1024]{1,0:T(1,128)}, u32[]{:S(2)}) copy-start(f32[1,1024]{1,0:T(1,128)} %get-tuple-element.95) | copy-start | bytes 12292
  276.2 7.5 %copy-start.9 = (f32[1,1024]{1,0:T(1,128)S(1)}, f32[1,1024]{1,0:T(1,128)}, u32[]{:S(2)}) copy-start(f32[1,1024]{1,0:T(1,128)} %get-tuple-element.140) | copy-start | bytes 12292
  276.2 7.5 %copy-start.10 = (f32[1,1024]{1,0:T(1,128)S(1)}, f32[1,1024]{1,0:T(1,128)}, u32[]{:S(2)}) copy-start(f32[1,1024]{1,0:T(1,128)} %get-tuple-element.142) | copy-start | bytes 12292
  276.2 7.5 %copy-start.11 = (f32[1,1024]{1,0:T(1,128)S(1)}, f32[1,1024]{1,0:T(1,128)}, u32[]{:S(2)}) copy-start(f32[1,1024]{1,0:T(1,128)} %get-tuple-element.87) | copy-start | bytes 12292
  276.2 7.5 %copy-start.12 = (f32[1,1024]{1,0:T(1,128)S(1)}, f32[1,1024]{1,0:T(1,128)}, u32[]{:S(2)}) copy-start(f32[1,1024]{1,0:T(1,128)} %get-tuple-element.89) | copy-start | bytes 12292
  276.2 7.5 %copy-start.13 = (f32[1,1024]{1,0:T(1,128)S(1)}, f32[1,1024]{1,0:T(1,128)}, u32[]{:S(2)}) copy-start(f32[1,1024]{1,0:T(1,128)} %get-tuple-element.143) | copy-start | bytes 12292
  276.2 7.5 %copy-start.14 = (f32[1,1024]{1,0:T(1,128)S(1)}, f32[1,1024]{1,0:T(1,128)}, u32[]{:S(2)}) copy-start(f32[1,1024]{1,0:T(1,128)} %get-tuple-element.145) | copy-start | bytes 12292
  361.6 11.4 %copy-start.6 = (f32[2,512]{1,0:T(2,128)S(1)}, f32[2,512]{1,0:T(2,128)}, u32[]{:S(2)}) copy-start(f32[2,512]{1,0:T(2,128)} %get-tuple-element.128) | copy-start | bytes 12292
  361.6 11.4 %copy-start.7 = (f32[2,512]{1,0:T(2,128)S(1)}, f32[2,512]{1,0:T(2,128)}, u32[]{:S(2)}) copy-start(f32[2,512]{1,0:T(2,128)} %get-tuple-element.129) | copy-start | bytes 12292
  390.4 34.0 %all-to-all-start.4 = ((bf16[2,512,1024]{2,0,1:T(2,128)(2,1)}), bf16[2,512,1024]{2,0,1:T(2,128)(2,1)S(1)}, u32[]{:S(2)}, u32[]{:S(2)}) async-start(bf16[2,512,1024]{2,0,1:T(2,128)(2,1)} %copy.48), calls=%async_computation.4 | async-start | bytes 4194304 | tf_op jit(solution)/shard_map/all_to_all | solution.py:181
  424.4 34.7 %all-to-all-start.3 = ((bf16[2,512,1024]{2,0,1:T(2,128)(2,1)}), bf16[2,512,1024]{2,0,1:T(2,128)(2,1)}, u32[]{:S(2)}, u32[]{:S(2)}) async-start(bf16[2,512,1024]{2,0,1:T(2,128)(2,1)} %copy.46), calls=%async_computation.3 | async-start | bytes 4194304 | tf_op jit(solution)/shard_map/all_to_all | solution.py:178
  431.1 119.2 %reduce-scatter.2.cloned.1.call-start = ((), (), s32[]{:S(2)}) async-start(), calls=%async_computation.7 | async-start | bytes 5242880 | tf_op jit(solution)/shard_map/reduce_scatter | solution.py:194
  470.8 24.2 %copy-start.1 = (f32[512,1,1024]{2,1,0:T(1,128)S(1)}, f32[512,1,1024]{2,1,0:T(1,128)}, u32[]{:S(2)}) copy-start(f32[512,1,1024]{2,1,0:T(1,128)} %get-tuple-element.40) | copy-start | bytes 6291460
  470.8 24.2 %copy-start.2 = (f32[512,1,1024]{2,1,0:T(1,128)S(1)}, f32[512,1,1024]{2,1,0:T(1,128)}, u32[]{:S(2)}) copy-start(f32[512,1,1024]{2,1,0:T(1,128)} %get-tuple-element.46) | copy-start | bytes 6291460
  470.8 24.2 %copy-start.16 = (f32[1024]{0:T(1024)S(1)}, f32[1024]{0:T(1024)}, u32[]{:S(2)}) copy-start(f32[1024]{0:T(1024)} %param.14) | copy-start | bytes 12292
Sparse Core Ops, SparseCore 0:
  504.9 45.3 reduce-scatter.1
where the time goes:
time: 563 us; the launch traced here: 557 us
  waiting for transfers between devices  152 us (27%)
  matrix products  140 us (25%)
  local copies, waits for them, and re-layouts  99.2 us (18%)
  other arithmetic  81 us (14%)
  starting transfers between devices  47.1 us (8%)
  blocking collectives  22.3 us (4%)
  between operations  15.6 us (3%)
    dot_general x12, matrix products, contract(): jnp.einsum(formula, left, right, precision=HIGHEST, preferred_element_typ...  130 us
    reduce_scatter x1, waiting for transfers between devices, shards(): lax.psum_scatter(jnp.dot(mixer, out_weight, preferred_element_type=jnp.fl...  45.6 us
    concatenate x1, other arithmetic, shards(): jnp.concatenate([extended[:rim_rows], seg_tokens, extended[3 * rim_rows:]...  41.5 us
    gather x1, local copies, waits for them, and re-layouts, shards(): picked = jnp.take(pool, pool_ids, axis=0).astype(jnp.float32)  27.2 us
    all_to_all x1, waiting for transfers between devices, shards(): lax.all_to_all(part_real.astype(jnp.bfloat16), 'seq', split_axis=0, conca...  23.4 us
    all_to_all x1, waiting for transfers between devices, shards(): lax.all_to_all(back_imag.astype(jnp.bfloat16), 'seq', split_axis=1, conca...  22.8 us
    all_to_all x1, blocking collectives, shards(): lax.all_to_all(pieces.astype(jnp.bfloat16), 'seq', split_axis=0, concat_a...  22.3 us
    all_to_all x1, waiting for transfers between devices, shards(): lax.all_to_all(back_real.astype(jnp.bfloat16), 'seq', split_axis=1, conca...  21.6 us
  transfers between devices with their start and end apart: 8, of which 7 were waited for; matrix products, arithmetic and copies ran while one was open for 9% of the time, Pallas kernels for 0%

commit v1 on v0

v1 whole, which is shorter than its diff:
```python
import functools

import jax
import jax.numpy as jnp
from jax import lax
from jax.experimental import pallas as pl
from jax.experimental.pallas import tpu as pltpu
from jax.sharding import PartitionSpec as P

F32 = jnp.float32
BF16 = jnp.bfloat16
LANES = 128
ROW_GROUP = 8
HEAD = 16
SUB = 4


def remote(src, dst, send_sem, recv_sem, **where):
    return pltpu.make_async_remote_copy(
        src_ref=src,
        dst_ref=dst,
        send_sem=send_sem,
        recv_sem=recv_sem,
        device_id=where,
        device_id_type=pl.DeviceIdType.MESH,
    )


def add_all(terms):
    while len(terms) > 1:
        terms = [a + b for a, b in zip(terms[::2], terms[1::2])] + (
            [terms[-1]] if len(terms) % 2 else []
        )
    return terms[0]


def kernel(
    n_seq,
    n_tp,
    len_ref,
    off_ref,
    x_hbm,
    taps_ref,
    res_ref,
    span_ref,
    skip_ref,
    w_hbm,
    out_ref,
    xq,
    xk,
    xv,
    w_ref,
    tail_out,
    tail_in,
    g_raw,
    f_raw,
    g_win,
    f_win,
    g_left,
    g_right,
    f_left,
    f_right,
    own_state,
    near_out,
    near_in,
    far_out,
    far_in,
    col_out,
    col_in,
    carry_ref,
    decay_t,
    weight_t,
    g_t,
    y_t,
    mix,
    cw_out,
    cw_in,
    ccw_out,
    ccw_in,
    load_sem,
    tail_ss,
    tail_rs,
    halo_ss,
    halo_rs,
    near_ss,
    near_rs,
    far_ss,
    far_rs,
    col_ss,
    col_rs,
    cw_ss,
    cw_rs,
    ccw_ss,
    ccw_rs,
):
    buf_rows = x_hbm.shape[1]
    rows = buf_rows // 2
    half = rows // 2
    chans = x_hbm.shape[2]
    modes = res_ref.shape[0]
    tiles = chans // LANES
    group = min(ROW_GROUP, n_seq)
    cols = n_seq // group
    s = lax.axis_index("seq")
    me = lax.axis_index("tp")
    row_id = lax.div(s, group)
    pos = lax.rem(s, group)

    def seq_at(k):
        return lax.rem(s + k + n_seq, n_seq)

    def mate(k):
        return row_id * group + lax.rem(pos + k, group)

    def below(k):
        return lax.rem(row_id + k, cols) * group + pos

    def tp_at(k):
        return lax.rem(me + k + n_tp, n_tp)

    loads = [
        pltpu.make_async_copy(x_hbm.at[j], ref.at[pl.ds(HEAD, buf_rows)], load_sem.at[j])
        for j, ref in ((1, xk), (2, xv), (0, xq))
    ]
    loads.append(pltpu.make_async_copy(w_hbm, w_ref, load_sem.at[3]))
    for copy in loads:
        copy.start()

    barrier = pltpu.get_barrier_semaphore()
    greeted = 0
    for k in (1, -1, 2, -2):
        pl.semaphore_signal(barrier, inc=1, device_id={"seq": seq_at(k)}, device_id_type=pl.DeviceIdType.MESH)
        greeted += 1
    for k in range(1, group):
        pl.semaphore_signal(barrier, inc=1, device_id={"seq": mate(k)}, device_id_type=pl.DeviceIdType.MESH)
        greeted += 1
    for k in range(1, cols):
        pl.semaphore_signal(barrier, inc=1, device_id={"seq": below(k)}, device_id_type=pl.DeviceIdType.MESH)
        greeted += 1
    for k in (1, -1):
        pl.semaphore_signal(barrier, inc=1, device_id={"tp": tp_at(k)}, device_id_type=pl.DeviceIdType.MESH)
        greeted += 1

    seg_len = len_ref[0]
    shift = off_ref[0] - (rows * s - half)

    for copy in loads[:3]:
        copy.wait()

    last_two = seg_len - 2 + lax.broadcasted_iota(jnp.int32, (HEAD, buf_rows), 0)
    have = lax.broadcasted_iota(jnp.int32, (HEAD, buf_rows), 1)
    pick_last = jnp.where(last_two == have, 1.0, 0.0).astype(BF16)
    for j, ref in enumerate((xq, xk, xv)):
        tail_out[pl.ds(2 * j, 2), :] = jnp.dot(
            pick_last, ref[pl.ds(HEAD, buf_rows), :], preferred_element_type=F32
        )[:2]
    tail_out[pl.ds(6, 2), :] = jnp.full((2, chans), jnp.minimum(seg_len, 2).astype(F32))

    pl.semaphore_wait(barrier, greeted)

    tails = [
        remote(tail_out, tail_in.at[k - 1], tail_ss.at[k - 1], tail_rs.at[k - 1], seq=seq_at(k))
        for k in (1, 2)
    ]
    for copy in tails:
        copy.start()
    def feature(ref, j, m, lane, width):
        block = ref[pl.ds(pl.multiple_of(16 * m, 16), 32), pl.ds(lane, width)].astype(F32)
        out = taps_ref[0, pl.ds(j, 1), pl.ds(lane, width)] * block[16:]
        for i in (1, 2):
            out += taps_ref[i, pl.ds(j, 1), pl.ds(lane, width)] * pltpu.roll(block, i, 0)[16:]
        return out

    width = 256

    def gate_rows(m, _):
        for lane in range(0, chans, width):
            gated = feature(xk, 1, m, lane, width) * feature(xv, 2, m, lane, width)
            g_raw[pl.ds(pl.multiple_of(16 * m, 16), 16), pl.ds(lane, width)] = gated.astype(BF16)
        return 0

    lax.fori_loop(1, buf_rows // 16, gate_rows, 0)

    for copy in tails:
        copy.wait_recv()
    count = tail_in[0, pl.ds(6, 1), :]
    row16 = lax.broadcasted_iota(jnp.int32, (HEAD, 1), 0)
    for j, ref in enumerate((xq, xk, xv)):
        prev_1, last_1 = tail_in[0, pl.ds(2 * j, 1), :], tail_in[0, pl.ds(2 * j + 1, 1), :]
        prev_2, last_2 = tail_in[1, pl.ds(2 * j, 1), :], tail_in[1, pl.ds(2 * j + 1, 1), :]
        prev_2, last_2 = jnp.where(s > 1, prev_2, 0.0), jnp.where(s > 1, last_2, 0.0)
        last = jnp.where(count > 0.5, last_1, last_2)
        prev = jnp.where(count > 1.5, prev_1, jnp.where(count > 0.5, last_2, prev_2))
        last, prev = jnp.where(s > 0, last, 0.0), jnp.where(s > 0, prev, 0.0)
        ref[pl.ds(0, HEAD), :] = jnp.where(
            row16 == HEAD - 1, last, jnp.where(row16 == HEAD - 2, prev, 0.0)
        ).astype(BF16)

    gate_rows(0, 0)

    def align(src, dst, b):
        first = max(0, b * LANES - rows)
        span = (b + 1) * LANES - first
        want = b * LANES - shift + lax.broadcasted_iota(jnp.int32, (LANES, span), 0)
        have = first + lax.broadcasted_iota(jnp.int32, (LANES, span), 1)
        pick = jnp.where((want == have) & (have < seg_len), 1.0, 0.0).astype(BF16)
        dst[pl.ds(b * LANES, LANES), :] = jnp.dot(
            pick, src[pl.ds(first, span), :], preferred_element_type=F32
        ).astype(BF16)

    def align_range(src, dst, first, stop):
        for b in range(first, stop):
            align(src, dst, b)

    side = half // LANES
    whole = buf_rows // LANES

    def window(src, dst, left, right, k):
        align_range(src, dst, 0, side)
        to_left = remote(
            dst.at[pl.ds(0, half)], right, halo_ss.at[k], halo_rs.at[k], seq=seq_at(-1)
        )
        to_left.start()
        align_range(src, dst, whole - side, whole)
        to_right = remote(
            dst.at[pl.ds(buf_rows - half, half)],
            left,
            halo_ss.at[k + 1],
            halo_rs.at[k + 1],
            seq=seq_at(1),
        )
        to_right.start()
        align_range(src, dst, side, whole - side)
        return [to_left, to_right]

    halos_g = window(g_raw, g_win, g_left, g_right, 0)

    sub8 = lax.broadcasted_iota(jnp.int32, (8, 1), 0).astype(F32)

    def states(j, _):
        lane = pl.ds(pl.multiple_of(j * LANES, LANES), LANES)
        rate = 1.0 / span_ref[:, lane]
        decay8 = jnp.exp(-8.0 * rate)
        step8 = [jnp.broadcast_to(decay8[r : r + 1], (8, LANES)) for r in range(modes)]

        def rows16(m, held):
            g = g_win[pl.ds(pl.multiple_of(16 * m, 16), 16), lane].astype(F32)
            held = [h * d + g[:8] for h, d in zip(held, step8)]
            return [h * d + g[8:] for h, d in zip(held, step8)]

        def put(ref, held):
            for r in range(modes):
                fold = jnp.exp((sub8 - 8.0) * rate[r : r + 1])
                ref[pl.ds(r, 1), lane] = jnp.sum(held[r] * fold, axis=0, keepdims=True)

        held = [jnp.zeros((8, LANES), F32)] * modes
        held = lax.fori_loop(0, half // 16, rows16, held)
        put(own_state, held)
        held = lax.fori_loop(half // 16, (half + rows) // 16, rows16, held)
        put(near_out, held)
        held = lax.fori_loop((half + rows) // 16, buf_rows // 16, rows16, held)
        put(far_out, held)
        return 0

    lax.fori_loop(0, tiles, states, 0)

    rate = 1.0 / span_ref[...]
    far_out[...] = far_out[...] * jnp.exp(float(half - rows) * rate)

    near = remote(near_out, near_in, near_ss, near_rs, seq=seq_at(1))
    near.start()
    fars = [
        remote(far_out, far_in.at[k - 1], far_ss.at[k - 1], far_rs.at[k - 1], seq=mate(k))
        for k in range(1, group)
    ]
    for copy in fars:
        copy.start()

    def query_rows(m, _):
        for lane in range(0, chans, width):
            f_raw[pl.ds(pl.multiple_of(16 * m, 16), 16), pl.ds(lane, width)] = feature(
                xq, 0, m, lane, width
            ).astype(BF16)
        return 0

    lax.fori_loop(0, buf_rows // 16, query_rows, 0)
    halos_f = window(f_raw, f_win, f_left, f_right, 2)

    def powers(blocks):
        return jnp.exp((-float(rows) * blocks.astype(F32)) * rate)

    for copy in fars:
        copy.wait_recv()
    carry = jnp.zeros_like(rate)
    row_sum = powers(group - 1 - pos) * far_out[...]
    row_short = jnp.where(
        pos < group - 1, powers(jnp.maximum(group - 2 - pos, 0)) * far_out[...], 0.0
    )
    for k in range(1, group):
        source = lax.rem(pos - k + group, group)
        piece = far_in[k - 1]
        row_sum += powers(group - 1 - source) * piece
        row_short += jnp.where(
            source < group - 1, powers(jnp.maximum(group - 2 - source, 0)) * piece, 0.0
        )
        if k >= 2:
            carry += jnp.where(k <= pos, powers(jnp.int32(k - 2)) * piece, 0.0)
    col_out[0] = jnp.where(pos == 0, row_short, powers(jnp.maximum(pos - 1, 0)) * row_sum)
    col_out[1] = powers(group + pos - 1) * row_sum
    downs = [
        remote(
            col_out.at[min(k - 1, 1)],
            col_in.at[k - 1],
            col_ss.at[k - 1],
            col_rs.at[k - 1],
            seq=below(k),
        )
        for k in range(1, cols)
    ]
    for copy in downs:
        copy.start()

    for copy in halos_g:
        copy.wait_recv()
    g_own = g_win.at[pl.ds(half, rows)]
    f_own = f_win.at[pl.ds(half, rows)]

    def join(own, left, right):
        def step(m, _):
            at = pl.ds(pl.multiple_of(16 * m, 16), 16)
            low = pl.ds(pl.multiple_of(half + 16 * m, 16), 16)
            high = pl.ds(pl.multiple_of(rows + 16 * m, 16), 16)
            own[low, :] = own[low, :] + left[at, :]
            own[high, :] = own[high, :] + right[at, :]
            return 0

        lax.fori_loop(0, half // 16, step, 0)

    join(g_win, g_left, g_right)
    decay1 = jnp.exp(-rate)
    weight = res_ref[...] * jnp.sqrt(rate)
    for j in range(tiles):
        decay_t[pl.ds(j, modes, stride=tiles), :] = decay1[:, j * LANES : (j + 1) * LANES]
        weight_t[pl.ds(j, modes, stride=tiles), :] = weight[:, j * LANES : (j + 1) * LANES]

    def spread(m, _):
        block = g_own[pl.ds(pl.multiple_of(16 * m, 16), 16), :].astype(F32)
        for j in range(tiles):
            g_t[pl.ds(16 * tiles * m + j, 16, stride=tiles), :] = block[
                :, j * LANES : (j + 1) * LANES
            ]
        return 0

    lax.fori_loop(0, rows // 16, spread, 0)

    decays = [decay_t[pl.ds(r * tiles, tiles), :] for r in range(modes)]
    weights = [weight_t[pl.ds(r * tiles, tiles), :] for r in range(modes)]

    def token(t, held):
        at = pl.ds(pl.multiple_of(t * tiles, tiles), tiles)
        g = g_t[at, :]
        held = [h * d + g for h, d in zip(held, decays)]
        y_t[at, :] = add_all([h * w for h, w in zip(held, weights)])
        return held

    lax.fori_loop(0, rows, token, [jnp.zeros((tiles, LANES), F32)] * modes, unroll=4)

    near.wait_recv()
    carry += own_state[...]
    carry += jnp.where(s > 0, near_in[...], 0.0)
    for k, copy in enumerate(downs, 1):
        copy.wait_recv()
        piece = col_in[k - 1]
        if k > 2:
            piece = piece * jnp.exp(-float(rows * group * (k - 2)) * rate)
        carry += jnp.where(k <= row_id, piece, 0.0)
    carry_ref[...] = carry * weight

    for copy in halos_f:
        copy.wait_recv()
    join(f_win, f_left, f_right)
    loads[3].wait()

    block_rows = rows // n_tp

    def mix_block(d):
        first = d * block_rows

        def tile(j, _):
            lane = pl.ds(pl.multiple_of(j * LANES, LANES), LANES)
            rate_j = 1.0 / span_ref[:, lane]
            decay8 = jnp.exp(-8.0 * rate_j)
            state = carry_ref[:, lane]
            skip = skip_ref[:, lane]
            ahead = sub8 + first.astype(F32)
            parts = [
                state[r : r + 1] * jnp.exp(-ahead * rate_j[r : r + 1]) for r in range(modes)
            ]
            step8 = [jnp.broadcast_to(decay8[r : r + 1], (8, LANES)) for r in range(modes)]

            def rows16(m, parts):
                row = pl.multiple_of(first + 16 * m, 16)
                g = g_own[pl.ds(row, 16), lane].astype(F32)
                f = f_own[pl.ds(row, 16), lane].astype(F32)
                done = []
                for k in range(2):
                    local = y_t[pl.ds((row + 8 * k) * tiles + j, 8, stride=tiles), :]
                    conv = local + add_all(parts)
                    done.append(f[8 * k : 8 * k + 8] * (conv + skip * g[8 * k : 8 * k + 8]))
                    parts = [p * d8 for p, d8 in zip(parts, step8)]
                mix[pl.ds(row, 16), lane] = jnp.concatenate(done, axis=0).astype(BF16)
                return parts

            lax.fori_loop(0, block_rows // 16, rows16, parts)
            return 0

        lax.fori_loop(0, tiles, tile, 0)

    out_cols = w_hbm.shape[1]
    piece_cols = out_cols // (2 * SUB)

    def partial(d, col):
        return jnp.dot(
            mix[pl.ds(pl.multiple_of(d * block_rows, block_rows), block_rows), :],
            w_ref[:, pl.ds(pl.multiple_of(col, piece_cols), piece_cols)],
            preferred_element_type=F32,
        )

    def ring(k, n, sign):
        out, into, ss, rs = (
            (cw_out, cw_in, cw_ss, cw_rs) if sign > 0 else (ccw_out, ccw_in, ccw_ss, ccw_rs)
        )
        return remote(
            out.at[k, n], into.at[k, n], ss.at[k, n], rs.at[k, n], tp=tp_at(sign)
        )

    for k in range(n_tp):
        if k == 0:
            mix_block(tp_at(-1))
            mix_block(tp_at(1))
        elif k == 1:
            mix_block(tp_at(2))
        elif k == 3:
            mix_block(me)

        def pieces(n, _, k=k):
            for sign, out, into in ((1, cw_out, cw_in), (-1, ccw_out, ccw_in)):
                col = n * piece_cols + (0 if sign > 0 else SUB * piece_cols)
                total = partial(tp_at(-sign * (k + 1)), col)
                if k > 0:
                    ring(k - 1, n, sign).wait_recv()
                    total += into[k - 1, n].astype(F32)
                if k < n_tp - 1:
                    out[k, n] = total.astype(BF16)
                    ring(k, n, sign).start()
                else:
                    out_ref[:, pl.ds(pl.multiple_of(col, piece_cols), piece_cols)] = total.astype(
                        BF16
                    )
            return 0

        lax.fori_loop(0, SUB, pieces, 0)

    for copy in tails + halos_g + halos_f + [near] + fars + downs:
        copy.wait_send()
    for k in range(n_tp - 1):

        def drain(n, _, k=k):
            ring(k, n, 1).wait_send()
            ring(k, n, -1).wait_send()
            return 0

        lax.fori_loop(0, SUB, drain, 0)


def shards(
    n_seq, n_tp, tokens, seg_length, seg_offset, short_weight, residues, spans, skip_gain, out_weight
):
    buf_rows, _, chans = tokens.shape
    rows = buf_rows // 2
    half = rows // 2
    modes = residues.shape[0]
    tiles = chans // LANES
    group = min(ROW_GROUP, n_seq)
    cols = n_seq // group
    out_cols = out_weight.shape[1]
    block_rows = rows // n_tp
    vmem = pl.BlockSpec(memory_space=pltpu.VMEM)
    smem = pl.BlockSpec(memory_space=pltpu.SMEM)
    hbm = pl.BlockSpec(memory_space=pl.ANY)
    piece = (n_tp - 1, SUB, block_rows, out_cols // (2 * SUB))
    dma = pltpu.SemaphoreType.DMA
    return pl.pallas_call(
        functools.partial(kernel, n_seq, n_tp),
        out_shape=jax.ShapeDtypeStruct((block_rows, out_cols), BF16),
        in_specs=[smem, smem, hbm, vmem, vmem, vmem, vmem, hbm],
        out_specs=vmem,
        scratch_shapes=[
            pltpu.VMEM((HEAD + buf_rows, chans), BF16),
            pltpu.VMEM((HEAD + buf_rows, chans), BF16),
            pltpu.VMEM((HEAD + buf_rows, chans), BF16),
            pltpu.VMEM((chans, out_cols), BF16),
            pltpu.VMEM((8, chans), F32),
            pltpu.VMEM((2, 8, chans), F32),
            pltpu.VMEM((buf_rows, chans), BF16),
            pltpu.VMEM((buf_rows, chans), BF16),
            pltpu.VMEM((buf_rows, chans), BF16),
            pltpu.VMEM((buf_rows, chans), BF16),
            pltpu.VMEM((half, chans), BF16),
            pltpu.VMEM((half, chans), BF16),
            pltpu.VMEM((half, chans), BF16),
            pltpu.VMEM((half, chans), BF16),
            pltpu.VMEM((modes, chans), F32),
            pltpu.VMEM((modes, chans), F32),
            pltpu.VMEM((modes, chans), F32),
            pltpu.VMEM((modes, chans), F32),
            pltpu.VMEM((group - 1, modes, chans), F32),
            pltpu.VMEM((2, modes, chans), F32),
            pltpu.VMEM((cols - 1, modes, chans), F32),
            pltpu.VMEM((modes, chans), F32),
            pltpu.VMEM((modes * tiles, LANES), F32),
            pltpu.VMEM((modes * tiles, LANES), F32),
            pltpu.VMEM((rows * tiles, LANES), F32),
            pltpu.VMEM((rows * tiles, LANES), F32),
            pltpu.VMEM((rows, chans), BF16),
            pltpu.VMEM(piece, BF16),
            pltpu.VMEM(piece, BF16),
            pltpu.VMEM(piece, BF16),
            pltpu.VMEM(piece, BF16),
            dma((4,)),
            dma((2,)),
            dma((2,)),
            dma((4,)),
            dma((4,)),
            dma,
            dma,
            dma((group - 1,)),
            dma((group - 1,)),
            dma((cols - 1,)),
            dma((cols - 1,)),
            dma(piece[:2]),
            dma(piece[:2]),
            dma(piece[:2]),
            dma(piece[:2]),
        ],
        compiler_params=pltpu.CompilerParams(
            collective_id=0, has_side_effects=True, vmem_limit_bytes=56 * 1024 * 1024
        ),
        name="hyena_mixer",
    )(
        seg_length,
        seg_offset,
        jnp.transpose(tokens, (1, 0, 2)),
        short_weight,
        residues,
        spans,
        skip_gain[None, :],
        out_weight,
    )


def solution(mesh):
    in_specs = (
        P("seq", None, "tp"),
        P("seq"),
        P("seq"),
        P(None, None, "tp"),
        P(None, "tp"),
        P(None, "tp"),
        P("tp"),
        P("tp", None),
    )
    out_specs = P(("seq", "tp"), None)
    body = functools.partial(shards, mesh.shape["seq"], mesh.shape["tp"])
    return jax.shard_map(body, mesh=mesh, in_specs=in_specs, out_specs=out_specs, check_vma=False)
```

time: 563 us -> 87.6 us (0.16)
  waiting for transfers between devices: 152 us -> 0 us
  matrix products: 140 us -> 0 us
  local copies, waits for them, and re-layouts: 99.2 us -> 2.29 us
  Pallas kernels: 0 us -> 83.8 us
  other arithmetic: 81 us -> 0 us
  starting transfers between devices: 47.1 us -> 0 us
  blocking collectives: 22.3 us -> 0 us
  between operations: 15.6 us -> 1.3 us
    dot_general x13 -> x0, matrix products: 140 us -> none  [the longest x12 130 us: contract(): jnp.einsum(formula, left, right, precision=HIGHEST, preferred_element_typ...]
    all_to_all x5 -> x0, waiting for transfers between devices: 106 us -> none  [the longest x1 23.4 us: shards(): lax.all_to_all(part_real.astype(jnp.bfloat16), 'seq', split_axis=0, conca...]
    pallas_call x0 -> x1, Pallas kernels: none -> 83.8 us  [shards(): pl.pallas_call(functools.partial(kernel, n_seq, n_tp), out_shape=jax.Shap...]
    reduce_scatter x1 -> x0, waiting for transfers between devices: 45.6 us -> none  [shards(): lax.psum_scatter(jnp.dot(mixer, out_weight, preferred_element_type=jnp.fl...]
    gather x2 -> x0, local copies, waits for them, and re-layouts: 41.9 us -> none  [the longest x1 27.2 us: shards(): picked = jnp.take(pool, pool_ids, axis=0).astype(jnp.float32)]
    concatenate x1 -> x0, other arithmetic: 41.5 us -> none  [shards(): jnp.concatenate([extended[:rim_rows], seg_tokens, extended[3 * rim_rows:]...]
    all_to_all x5 -> x0, starting transfers between devices: 40.1 us -> none  [the longest x1 16.1 us: shards(): lax.all_to_all(gated.reshape(1, rows_here, channels), 'seq', split_axis=1...]
    all_to_all x1 -> x0, blocking collectives: 22.3 us -> none  [shards(): lax.all_to_all(pieces.astype(jnp.bfloat16), 'seq', split_axis=0, concat_a...]
  transfers between devices with their start and end apart: 8 -> 0, of which waited for: 7 -> 0; matrix products, arithmetic and copies ran while one was open for 9% -> 0% of each run, Pallas kernels for 0% -> 0%
where the time goes in v1:
time: 87.6 us; the launch traced here: 87.4 us
  Pallas kernels  83.8 us (96%)
  local copies, waits for them, and re-layouts  2.29 us (3%)
  between operations  1.3 us (1%)
    pallas_call x1, Pallas kernels, shards(): pl.pallas_call(functools.partial(kernel, n_seq, n_tp), out_shape=jax.Shap...  83.8 us
    unnamed x1, local copies, waits for them, and re-layouts  2.29 us

profile of v1, /device:TPU:1, one launch (start us, length us, event | category | flops | bytes accessed | tf_op | source)
XLA Modules:
  0.0 87.4 jit_solution(8034234537920170732)
XLA Ops:
  1.3 83.8 %hyena_mixer.1 = bf16[128,4096]{1,0:T(8,128)(2,1)} custom-call(s32[1]{0:T(128)S(6)} %copy.10.len_ref, s32[1]{0:T(128)S(6)} %copy.11.off_ref, bf16[3,1024,1024]{2,1,0:T(8,128)(2,1)} %bitcast.2, f32[3,3,1024]{2,1,0:T(4,128)} %taps_ref.1, f32[16,1024]{1,0:T(8,128)} %res_ref.1, f32[16,1024]{1,0:T(8,128)} %span_ref.1, f32[1,1024]{1,0:T(1,128)} %bitcast.3, ...), custom_call_target="tpu_custom_call" | custom-call | tf_op jit(solution)/shard_map/hyena_mixer/pallas_call | solution.py:493
  85.1 2.3 %copy.12 = bf16[128,4096]{1,0:T(8,128)(2,1)} copy(bf16[128,4096]{1,0:T(8,128)(2,1)} %hyena_mixer.1) | data formatting | bytes 2097152

commit v2 on v1

v2 whole, which is shorter than its diff:
```python
import functools

import jax
import jax.numpy as jnp
from jax import lax
from jax.experimental import pallas as pl
from jax.experimental.pallas import tpu as pltpu
from jax.sharding import PartitionSpec as P

F32 = jnp.float32
BF16 = jnp.bfloat16
LANES = 128
ROW_GROUP = 8
HEAD = 8
CHUNK = 64
SUB = 4


def remote(src, dst, send_sem, recv_sem, **where):
    return pltpu.make_async_remote_copy(
        src_ref=src,
        dst_ref=dst,
        send_sem=send_sem,
        recv_sem=recv_sem,
        device_id=where,
        device_id_type=pl.DeviceIdType.MESH,
    )


def add_all(terms):
    while len(terms) > 1:
        terms = [a + b for a, b in zip(terms[::2], terms[1::2])] + (
            [terms[-1]] if len(terms) % 2 else []
        )
    return terms[0]


def kernel(
    n_seq,
    n_tp,
    len_ref,
    off_ref,
    x_hbm,
    taps_ref,
    res_ref,
    span_ref,
    skip_ref,
    w_hbm,
    out_ref,
    xq,
    xk,
    xv,
    w_ref,
    q_t,
    k_t,
    v_t,
    taps_t,
    tail_out,
    tail_in,
    qtail_out,
    qtail_in,
    g_t,
    f_t,
    g_out,
    g_in,
    f_out,
    f_in,
    own_state,
    near_out,
    near_in,
    far_out,
    far_in,
    col_out,
    col_in,
    carry_ref,
    rate_t,
    weight_t,
    skip_t,
    y_t,
    mix,
    cw_out,
    cw_in,
    ccw_out,
    ccw_in,
    load_sem,
    tail_ss,
    tail_rs,
    qtail_ss,
    qtail_rs,
    halo_ss,
    halo_rs,
    near_ss,
    near_rs,
    far_ss,
    far_rs,
    col_ss,
    col_rs,
    cw_ss,
    cw_rs,
    ccw_ss,
    ccw_rs,
):
    buf_rows = x_hbm.shape[1]
    rows = buf_rows // 2
    half = rows // 2
    chans = x_hbm.shape[2]
    modes = res_ref.shape[0]
    tiles = chans // LANES
    group = min(ROW_GROUP, n_seq)
    cols = n_seq // group
    s = lax.axis_index("seq")
    me = lax.axis_index("tp")
    row_id = lax.div(s, group)
    pos = lax.rem(s, group)

    def seq_at(k):
        return lax.rem(s + k + n_seq, n_seq)

    def mate(k):
        return row_id * group + lax.rem(pos + k, group)

    def below(k):
        return lax.rem(row_id + k, cols) * group + pos

    def tp_at(k):
        return lax.rem(me + k + n_tp, n_tp)

    loads = [
        pltpu.make_async_copy(x_hbm.at[j], ref, load_sem.at[j])
        for j, ref in ((1, xk), (2, xv), (0, xq))
    ]
    loads.append(pltpu.make_async_copy(w_hbm, w_ref, load_sem.at[3]))
    for copy in loads:
        copy.start()

    barrier = pltpu.get_barrier_semaphore()
    greeted = 0
    for k in (1, -1, 2, -2):
        pl.semaphore_signal(barrier, inc=1, device_id={"seq": seq_at(k)}, device_id_type=pl.DeviceIdType.MESH)
        greeted += 1
    for k in range(1, group):
        pl.semaphore_signal(barrier, inc=1, device_id={"seq": mate(k)}, device_id_type=pl.DeviceIdType.MESH)
        greeted += 1
    for k in range(1, cols):
        pl.semaphore_signal(barrier, inc=1, device_id={"seq": below(k)}, device_id_type=pl.DeviceIdType.MESH)
        greeted += 1
    for k in (1, -1):
        pl.semaphore_signal(barrier, inc=1, device_id={"tp": tp_at(k)}, device_id_type=pl.DeviceIdType.MESH)
        greeted += 1

    seg_len = jnp.clip(len_ref[0], 0, buf_rows)
    shift = jnp.clip(off_ref[0] - (rows * s - half), 0, rows)

    for j in range(tiles):
        lane = pl.ds(j * LANES, LANES)
        rate = 1.0 / span_ref[:, lane]
        rate_t[:, j, :] = rate
        weight_t[:, j, :] = res_ref[:, lane] * jnp.sqrt(rate)
        skip_t[pl.ds(j, 1), :] = skip_ref[:, lane]
        for i in range(3):
            for n in range(3):
                taps_t[3 * n + i, pl.ds(j, 1), :] = taps_ref[i, pl.ds(n, 1), lane]
    pad = rows + HEAD
    for ref in (k_t, v_t, q_t):
        ref[pl.ds(0, pad)] = jnp.zeros((pad, tiles, LANES), F32)

    def spread(copy, src, dst):
        copy.wait()

        def step(m, _):
            for j in range(tiles):
                dst[pl.ds(pad + CHUNK * m, CHUNK), j, :] = src[
                    pl.ds(pl.multiple_of(CHUNK * m, CHUNK), CHUNK), pl.ds(j * LANES, LANES)
                ].astype(F32)
            return 0

        lax.fori_loop(0, buf_rows // CHUNK, step, 0)

    def send_tails(out, into, ss, rs):
        copies = [
            remote(out, into.at[k - 1], ss.at[k - 1], rs.at[k - 1], seq=seq_at(k)) for k in (1, 2)
        ]
        for copy in copies:
            copy.start()
        return copies

    spread(loads[0], xk, k_t)
    spread(loads[1], xv, v_t)
    tail_out[4] = jnp.full((tiles, LANES), jnp.minimum(seg_len, 2).astype(F32))
    for n, ref in enumerate((k_t, v_t)):
        for k in range(2):
            tail_out[2 * n + k] = ref[pad - 2 + k + seg_len]
    pl.semaphore_wait(barrier, greeted)
    tails = send_tails(tail_out, tail_in, tail_ss, tail_rs)
    spread(loads[2], xq, q_t)
    for k in range(2):
        qtail_out[k] = q_t[pad - 2 + k + seg_len]
    qtails = send_tails(qtail_out, qtail_in, qtail_ss, qtail_rs)

    def put_tail(dst, into, n):
        count = tail_in[0, 4]
        last = jnp.where(count > 0.5, into[0, 2 * n + 1], jnp.where(s > 1, into[1, 2 * n + 1], 0.0))
        prev = jnp.where(
            count > 1.5,
            into[0, 2 * n],
            jnp.where(s > 1, jnp.where(count > 0.5, into[1, 2 * n + 1], into[1, 2 * n]), 0.0),
        )
        dst[pad - 1] = jnp.where(s > 0, last, 0.0)
        dst[pad - 2] = jnp.where(s > 0, prev, 0.0)

    reach = 0.5 * seg_len.astype(F32)
    middle = reach - 0.5 + shift.astype(F32)

    def pairs_of(first, stop, sources, store):
        def load(ref, u):
            return ref[pad - shift + u]

        def step(v, held):
            away, *past = held
            u = 2 * v
            values = []
            later = []
            for (ref, taps), (before, last) in zip(sources, past):
                x = [before, last, load(ref, u), load(ref, u + 1)]
                values.append(
                    [taps[0] * x[k + 2] + taps[1] * x[k + 1] + taps[2] * x[k] for k in range(2)]
                )
                later.append((x[2], x[3]))
            kept = []
            for k in range(2):
                value = values[0][k]
                for other in values[1:]:
                    value = value * other[k]
                kept.append(jnp.where(jnp.abs(away + k) < reach, value, 0.0))
            store(u, kept)
            return (away + 2.0, *later)

        away = jnp.zeros((tiles, LANES), F32) + (first - middle)
        past = [(load(ref, first - 2), load(ref, first - 1)) for ref, _ in sources]
        lax.fori_loop(first // 2, stop // 2, step, (away, *past), unroll=4)

    taps = [[taps_t[3 * n + i] for i in range(3)] for n in range(3)]

    def gate(first, stop, at=None):
        def store(u, kept):
            pair = jnp.concatenate(kept, axis=0).astype(BF16)
            if at is not None:
                place = pl.multiple_of((u - first + at) * tiles, 2 * tiles)
                g_out[pl.ds(place, 2 * tiles), :] = pair
            wide = pair.astype(F32)
            g_t[u] = wide[:tiles]
            g_t[u + 1] = wide[tiles:]

        pairs_of(first, stop, [(k_t, taps[1]), (v_t, taps[2])], store)

    def query(first, stop, at=None):
        def store(u, kept):
            if at is not None:
                place = pl.multiple_of((u - first + at) * tiles, 2 * tiles)
                f_out[pl.ds(place, 2 * tiles), :] = jnp.concatenate(kept, axis=0).astype(BF16)
            else:
                f_t[u - half] = kept[0]
                f_t[u - half + 1] = kept[1]

        pairs_of(first, stop, [(q_t, taps[0])], store)

    def halo(out, into, k):
        size = half * tiles
        low, high = pl.ds(0, size), pl.ds(size, size)
        return [
            remote(out.at[low], into.at[low], halo_ss.at[k], halo_rs.at[k], seq=seq_at(1)),
            remote(
                out.at[high], into.at[high], halo_ss.at[k + 1], halo_rs.at[k + 1], seq=seq_at(-1)
            ),
        ]

    halos_g = halo(g_out, g_in, 0)
    halos_f = halo(f_out, f_in, 2)
    free = rows + 8
    gate(half + rows, buf_rows, 0)
    halos_g[0].start()
    gate(free, half + rows)
    query(half + rows, buf_rows, 0)
    query(free, half + rows)
    for copy in tails:
        copy.wait_recv()
    put_tail(k_t, tail_in, 0)
    put_tail(v_t, tail_in, 1)
    gate(0, half, half)
    halos_g[1].start()
    gate(half, free)

    rate = rate_t[...]
    decay1 = jnp.exp(-rate)
    decays = [decay1[r] for r in range(modes)]

    def accumulate(u, held):
        g = g_t[u]
        return [h * d + g for h, d in zip(held, decays)]

    flat = (modes * tiles, LANES)
    shaped = (modes, tiles, LANES)
    held = [jnp.zeros((tiles, LANES), F32)] * modes
    held = lax.fori_loop(0, half, accumulate, held, unroll=8)
    for r in range(modes):
        own_state[r] = held[r] * decays[r]
    held = lax.fori_loop(half, half + rows, accumulate, held, unroll=8)
    near_out[...] = jnp.concatenate([h * d for h, d in zip(held, decays)], axis=0).astype(BF16)
    held = lax.fori_loop(half + rows, buf_rows, accumulate, held, unroll=8)
    ahead = jnp.exp(float(half - rows - 1) * rate)
    whole = jnp.concatenate([held[r] * ahead[r] for r in range(modes)], axis=0).astype(BF16)
    far_out[...] = whole

    fars = [
        remote(far_out, far_in.at[k - 1], far_ss.at[k - 1], far_rs.at[k - 1], seq=mate(k))
        for k in range(1, group)
    ]
    for copy in fars:
        copy.start()
    near = remote(near_out, near_in, near_ss, near_rs, seq=seq_at(1))
    near.start()

    for copy in qtails:
        copy.wait_recv()
    put_tail(q_t, qtail_in, 0)
    query(0, half, half)
    query(half, free)
    for copy in fars:
        copy.wait_send()
    for copy in halos_f:
        copy.start()

    for copy in halos_g:
        copy.wait_recv()
    weights = [weight_t[r] for r in range(modes)]
    skip = skip_t[...]

    def pair_of(src, into, u):
        other = into[pl.ds(pl.multiple_of(u * tiles, 2 * tiles), 2 * tiles), :].astype(F32)
        return src[u] + other[:tiles], src[u + 1] + other[tiles:]

    def tokens(v, held):
        for k, g in enumerate(pair_of(g_t.at[pl.ds(half, rows)], g_in, 2 * v)):
            held = [h * d + g for h, d in zip(held, decays)]
            y_t[2 * v + k] = add_all([h * w for h, w in zip(held, weights)] + [skip * g])
        return held

    local = [jnp.zeros((tiles, LANES), F32)] * modes
    local = lax.fori_loop(0, rows // 4, tokens, local, unroll=2)

    def powers(blocks):
        return jnp.exp((-float(rows) * blocks.astype(F32)) * rate)

    for copy in fars:
        copy.wait_recv()
    carry = jnp.zeros_like(rate)
    mine = far_out[...].astype(F32).reshape(shaped)
    row_sum = powers(group - 1 - pos) * mine
    row_short = jnp.where(
        pos < group - 1, powers(jnp.maximum(group - 2 - pos, 0)) * mine, 0.0
    )
    for k in range(1, group):
        source = lax.rem(pos - k + group, group)
        piece = far_in[k - 1].astype(F32).reshape(shaped)
        row_sum += powers(group - 1 - source) * piece
        row_short += jnp.where(
            source < group - 1, powers(jnp.maximum(group - 2 - source, 0)) * piece, 0.0
        )
        if k >= 2:
            carry += jnp.where(k <= pos, powers(jnp.int32(k - 2)) * piece, 0.0)
    first_down = jnp.where(pos == 0, row_short, powers(jnp.maximum(pos - 1, 0)) * row_sum)
    col_out[0] = first_down.reshape(flat).astype(BF16)
    col_out[1] = (powers(group + pos - 1) * row_sum).reshape(flat).astype(BF16)
    downs = [
        remote(
            col_out.at[min(k - 1, 1)],
            col_in.at[k - 1],
            col_ss.at[k - 1],
            col_rs.at[k - 1],
            seq=below(k),
        )
        for k in range(1, cols)
    ]
    for copy in downs:
        copy.start()

    lax.fori_loop(rows // 4, rows // 2, tokens, local, unroll=2)

    near.wait_recv()
    carry += own_state[...]
    carry += jnp.where(s > 0, near_in[...].astype(F32).reshape(shaped), 0.0)
    for k, copy in enumerate(downs, 1):
        copy.wait_recv()
        piece = col_in[k - 1].astype(F32).reshape(shaped)
        if k > 2:
            piece = piece * jnp.exp(-float(rows * group * (k - 2)) * rate)
        carry += jnp.where(k <= row_id, piece, 0.0)
    carry_ref[...] = carry * weight_t[...]

    for copy in halos_f:
        copy.wait_recv()
    loads[3].wait()

    block_rows = rows // n_tp

    def mix_block(d):
        first = d * block_rows
        ahead = jnp.exp(-first.astype(F32) * rate_t[...])
        parts = [carry_ref[r] * ahead[r] for r in range(modes)]

        def pairs(v, parts):
            u = first + 2 * v
            for k, f in enumerate(pair_of(f_t, f_in, u)):
                y_t[u + k] = f * add_all(parts + [y_t[u + k]])
                parts = [p * d1 for p, d1 in zip(parts, decays)]
            return parts

        lax.fori_loop(0, block_rows // 2, pairs, parts, unroll=2)

        def lay(m, _):
            row = pl.multiple_of(first + 16 * m, 16)
            for j in range(tiles):
                mix[pl.ds(row, 16), pl.ds(j * LANES, LANES)] = y_t[pl.ds(row, 16), j, :].astype(
                    BF16
                )
            return 0

        lax.fori_loop(0, block_rows // 16, lay, 0, unroll=2)

    out_cols = w_hbm.shape[1]
    piece_cols = out_cols // (2 * SUB)

    def partial(d, col):
        return jnp.dot(
            mix[pl.ds(pl.multiple_of(d * block_rows, block_rows), block_rows), :],
            w_ref[:, pl.ds(pl.multiple_of(col, piece_cols), piece_cols)],
            preferred_element_type=F32,
        )

    def ring(k, n, sign):
        out, into, ss, rs = (
            (cw_out, cw_in, cw_ss, cw_rs) if sign > 0 else (ccw_out, ccw_in, ccw_ss, ccw_rs)
        )
        return remote(
            out.at[k, n], into.at[k, n], ss.at[k, n], rs.at[k, n], tp=tp_at(sign)
        )

    for k in range(n_tp):

        def pieces(n, _, k=k, signs=(1, -1)):
            for sign in signs:
                out, into = (cw_out, cw_in) if sign > 0 else (ccw_out, ccw_in)
                col = n * piece_cols + (0 if sign > 0 else SUB * piece_cols)
                total = partial(tp_at(-sign * (k + 1)), col)
                if k > 0:
                    ring(k - 1, n, sign).wait_recv()
                    total += into[k - 1, n].astype(F32)
                if k < n_tp - 1:
                    out[k, n] = total.astype(BF16)
                    ring(k, n, sign).start()
                else:
                    out_ref[:, pl.ds(pl.multiple_of(col, piece_cols), piece_cols)] = total.astype(
                        BF16
                    )
            return 0

        if k == 0:
            mix_block(tp_at(-1))
            pieces(0, 0, signs=(1,))
            mix_block(tp_at(1))
            pieces(0, 0, signs=(-1,))
            lax.fori_loop(1, SUB, pieces, 0)
            mix_block(tp_at(2))
        else:
            lax.fori_loop(0, SUB, pieces, 0)
            if k == 1:
                mix_block(me)

    for copy in tails + qtails + halos_g + halos_f + [near] + downs:
        copy.wait_send()
    for k in range(n_tp - 1):

        def drain(n, _, k=k):
            ring(k, n, 1).wait_send()
            ring(k, n, -1).wait_send()
            return 0

        lax.fori_loop(0, SUB, drain, 0)


def shards(
    n_seq, n_tp, tokens, seg_length, seg_offset, short_weight, residues, spans, skip_gain, out_weight
):
    buf_rows, _, chans = tokens.shape
    rows = buf_rows // 2
    modes = residues.shape[0]
    tiles = chans // LANES
    group = min(ROW_GROUP, n_seq)
    cols = n_seq // group
    out_cols = out_weight.shape[1]
    block_rows = rows // n_tp
    vmem = pl.BlockSpec(memory_space=pltpu.VMEM)
    smem = pl.BlockSpec(memory_space=pltpu.SMEM)
    hbm = pl.BlockSpec(memory_space=pl.ANY)
    piece = (n_tp - 1, SUB, block_rows, out_cols // (2 * SUB))
    dma = pltpu.SemaphoreType.DMA
    state = (modes, tiles, LANES)
    flat = (modes * tiles, LANES)
    return pl.pallas_call(
        functools.partial(kernel, n_seq, n_tp),
        out_shape=jax.ShapeDtypeStruct((block_rows, out_cols), BF16),
        in_specs=[smem, smem, hbm, vmem, vmem, vmem, vmem, hbm],
        out_specs=vmem,
        scratch_shapes=[
            pltpu.VMEM((buf_rows, chans), BF16),
            pltpu.VMEM((buf_rows, chans), BF16),
            pltpu.VMEM((buf_rows, chans), BF16),
            pltpu.VMEM((chans, out_cols), BF16),
            pltpu.VMEM((rows + HEAD + buf_rows, tiles, LANES), F32),
            pltpu.VMEM((rows + HEAD + buf_rows, tiles, LANES), F32),
            pltpu.VMEM((rows + HEAD + buf_rows, tiles, LANES), F32),
            pltpu.VMEM((9, tiles, LANES), F32),
            pltpu.VMEM((5, tiles, LANES), F32),
            pltpu.VMEM((2, 5, tiles, LANES), F32),
            pltpu.VMEM((2, tiles, LANES), F32),
            pltpu.VMEM((2, 2, tiles, LANES), F32),
            pltpu.VMEM((buf_rows, tiles, LANES), F32),
            pltpu.VMEM((rows, tiles, LANES), F32),
            pltpu.VMEM((rows * tiles, LANES), BF16),
            pltpu.VMEM((rows * tiles, LANES), BF16),
            pltpu.VMEM((rows * tiles, LANES), BF16),
            pltpu.VMEM((rows * tiles, LANES), BF16),
            pltpu.VMEM(state, F32),
            pltpu.VMEM(flat, BF16),
            pltpu.VMEM(flat, BF16),
            pltpu.VMEM(flat, BF16),
            pltpu.VMEM((group - 1, *flat), BF16),
            pltpu.VMEM((2, *flat), BF16),
            pltpu.VMEM((cols - 1, *flat), BF16),
            pltpu.VMEM(state, F32),
            pltpu.VMEM(state, F32),
            pltpu.VMEM(state, F32),
            pltpu.VMEM((tiles, LANES), F32),
            pltpu.VMEM((rows, tiles, LANES), F32),
            pltpu.VMEM((rows, chans), BF16),
            pltpu.VMEM(piece, BF16),
            pltpu.VMEM(piece, BF16),
            pltpu.VMEM(piece, BF16),
            pltpu.VMEM(piece, BF16),
            dma((4,)),
            dma((2,)),
            dma((2,)),
            dma((2,)),
            dma((2,)),
            dma((4,)),
            dma((4,)),
            dma,
            dma,
            dma((group - 1,)),
            dma((group - 1,)),
            dma((cols - 1,)),
            dma((cols - 1,)),
            dma(piece[:2]),
            dma(piece[:2]),
            dma(piece[:2]),
            dma(piece[:2]),
        ],
        compiler_params=pltpu.CompilerParams(
            collective_id=0, has_side_effects=True, vmem_limit_bytes=60 * 1024 * 1024
        ),
        name="hyena_mixer",
    )(
        seg_length,
        seg_offset,
        jnp.transpose(tokens, (1, 0, 2)),
        short_weight,
        residues,
        spans,
        skip_gain[None, :],
        out_weight,
    )


def solution(mesh):
    in_specs = (
        P("seq", None, "tp"),
        P("seq"),
        P("seq"),
        P(None, None, "tp"),
        P(None, "tp"),
        P(None, "tp"),
        P("tp"),
        P("tp", None),
    )
    out_specs = P(("seq", "tp"), None)
    body = functools.partial(shards, mesh.shape["seq"], mesh.shape["tp"])
    return jax.shard_map(body, mesh=mesh, in_specs=in_specs, out_specs=out_specs, check_vma=False)
```

time: 87.6 us -> 82.6 us (0.943)
  Pallas kernels: 83.8 us -> 78.8 us
    pallas_call x1, Pallas kernels: 83.8 us -> 78.8 us  [shards(): pl.pallas_call(functools.partial(kernel, n_seq, n_tp), out_shape=jax.Shap...]
where the time goes in v2:
time: 82.6 us; the launch traced here: 82.4 us
  Pallas kernels  78.8 us (95%)
  local copies, waits for them, and re-layouts  2.29 us (3%)
  between operations  1.3 us (2%)
    pallas_call x1, Pallas kernels, shards(): pl.pallas_call(functools.partial(kernel, n_seq, n_tp), out_shape=jax.Shap...  78.8 us
    unnamed x1, local copies, waits for them, and re-layouts  2.29 us

profile of v2, /device:TPU:1, one launch (start us, length us, event | category | flops | bytes accessed | tf_op | source)
XLA Modules:
  0.0 82.4 jit_solution(9255667631359897293)
XLA Ops:
  1.3 78.8 %hyena_mixer.1 = bf16[128,4096]{1,0:T(8,128)(2,1)} custom-call(s32[1]{0:T(128)S(6)} %copy.10.len_ref, s32[1]{0:T(128)S(6)} %copy.11.off_ref, bf16[3,1024,1024]{2,1,0:T(8,128)(2,1)} %bitcast.2, f32[3,3,1024]{2,1,0:T(4,128)} %taps_ref.1, f32[16,1024]{1,0:T(8,128)} %res_ref.1, f32[16,1024]{1,0:T(8,128)} %span_ref.1, f32[1,1024]{1,0:T(1,128)} %bitcast.3, ...), custom_call_target="tpu_custom_call" | custom-call | tf_op jit(solution)/shard_map/hyena_mixer/pallas_call | solution.py:509
  80.1 2.3 %copy.12 = bf16[128,4096]{1,0:T(8,128)(2,1)} copy(bf16[128,4096]{1,0:T(8,128)(2,1)} %hyena_mixer.1) | data formatting | bytes 2097152

commit v3 on v2

v3 whole, which is shorter than its diff:
```python
import functools

import jax
import jax.numpy as jnp
from jax import lax
from jax.experimental import pallas as pl
from jax.experimental.pallas import tpu as pltpu
from jax.sharding import PartitionSpec as P

F32 = jnp.float32
BF16 = jnp.bfloat16
LANES = 128
ROW_GROUP = 8
HEAD = 8
FEW = 4
BATCH = 8
CHUNK = 32
SUB = 4
FLIGHT = 2


def remote(src, dst, send_sem, recv_sem, **where):
    return pltpu.make_async_remote_copy(
        src_ref=src,
        dst_ref=dst,
        send_sem=send_sem,
        recv_sem=recv_sem,
        device_id=where,
        device_id_type=pl.DeviceIdType.MESH,
    )


def add_all(terms):
    while len(terms) > 1:
        terms = [a + b for a, b in zip(terms[::2], terms[1::2])] + (
            [terms[-1]] if len(terms) % 2 else []
        )
    return terms[0]


def kernel(
    n_seq,
    n_tp,
    len_ref,
    off_ref,
    x_hbm,
    taps_ref,
    res_ref,
    span_ref,
    skip_ref,
    w_hbm,
    out_ref,
    x_ref,
    w_ref,
    x_t,
    taps_t,
    tail_out,
    tail_in,
    g_win,
    g_in,
    f_win,
    f_in,
    snaps,
    near_out,
    near_in,
    far_out,
    far_in,
    sums,
    col_out,
    col_in,
    carry_ref,
    rate_t,
    weight_t,
    skip_t,
    y_t,
    mix,
    ring_out,
    ring_in,
    load_sem,
    tail_ss,
    tail_rs,
    halo_ss,
    halo_rs,
    near_ss,
    near_rs,
    far_ss,
    far_rs,
    col_ss,
    col_rs,
    ring_ss,
    ring_rs,
):
    buf_rows = x_hbm.shape[1]
    rows = buf_rows // 2
    half = rows // 2
    chans = x_hbm.shape[2]
    modes = res_ref.shape[0]
    tiles = chans // LANES
    group = min(ROW_GROUP, n_seq)
    cols = n_seq // group
    pad = rows + HEAD
    flat = (modes * tiles, LANES)
    shaped = (modes, tiles, LANES)
    s = lax.axis_index("seq")
    me = lax.axis_index("tp")
    row_id = lax.div(s, group)
    pos = lax.rem(s, group)

    def seq_at(k):
        return lax.rem(s + k + n_seq, n_seq)

    def mate(k):
        return row_id * group + lax.rem(pos + k, group)

    def below(k):
        return lax.rem(row_id + k, cols) * group + pos

    def tp_at(k):
        return lax.rem(me + k + n_tp, n_tp)

    loads = [
        pltpu.make_async_copy(x_hbm.at[n], x_ref.at[n], load_sem.at[n]) for n in range(3)
    ]
    loads.append(pltpu.make_async_copy(w_hbm, w_ref, load_sem.at[3]))
    for n in (1, 2, 0):
        loads[n].start()

    barrier = pltpu.get_barrier_semaphore()

    def greet(**where):
        pl.semaphore_signal(barrier, inc=1, device_id=where, device_id_type=pl.DeviceIdType.MESH)

    for k in (1, -1, 2, -2):
        greet(seq=seq_at(k))
    for k in range(1, group):
        greet(seq=mate(k))
    for k in range(1, cols):
        greet(seq=below(k))
    for k in (1, -1):
        greet(tp=tp_at(k))

    seg_len = jnp.clip(len_ref[0], 0, buf_rows)
    shift = jnp.clip(off_ref[0] - (rows * s - half), 0, rows)

    for j in range(tiles):
        lane = pl.ds(j * LANES, LANES)
        rate = 1.0 / span_ref[:, lane]
        rate_t[:, j, :] = rate
        weight_t[:, j, :] = res_ref[:, lane] * jnp.sqrt(rate)
        skip_t[pl.ds(j, 1), :] = skip_ref[:, lane]
        for i in range(3):
            for n in range(3):
                taps_t[3 * n + i, pl.ds(j, 1), :] = taps_ref[i, pl.ds(n, 1), lane]

    def clear(m, _):
        for n in range(3):
            x_t[n, pl.ds(HEAD * m, HEAD)] = jnp.zeros((HEAD, tiles, LANES), F32)
        return 0

    lax.fori_loop(0, pad // HEAD, clear, 0)
    piece_rows, piece_cols = ring_in.shape[3:]

    def clear_ring(m, _):
        for sign in range(2):
            for n in range(SUB):
                ring_in[sign, 0, n, pl.ds(pl.multiple_of(16 * m, 16), 16)] = jnp.zeros(
                    (16, piece_cols), BF16
                )
        return 0

    lax.fori_loop(0, piece_rows // 16, clear_ring, 0)

    def spread(t, _):
        n, m = lax.div(t, buf_rows // CHUNK), lax.rem(t, buf_rows // CHUNK)
        block = x_ref[n, pl.ds(pl.multiple_of(CHUNK * m, CHUNK), CHUNK), :].astype(F32)
        x_t[n, pl.ds(pad + CHUNK * m, CHUNK)] = block.reshape(CHUNK, tiles, LANES)
        return 0

    def send_tails(part, k):
        copies = [
            remote(
                tail_out.at[part],
                tail_in.at[i, part],
                tail_ss.at[k + i],
                tail_rs.at[k + i],
                seq=seq_at(i + 1),
            )
            for i in range(2)
        ]
        for copy in copies:
            copy.start()
        return copies

    starts = (5, 0, 2)
    chunks = buf_rows // CHUNK
    loads[1].wait()
    loads[2].wait()
    lax.fori_loop(chunks, 3 * chunks, spread, 0)
    for n in (1, 2):
        for k in range(2):
            tail_out[starts[n] + k] = x_t[n, pad - 2 + k + seg_len]
    tail_out[4] = jnp.full((tiles, LANES), jnp.minimum(seg_len, 2).astype(F32))
    pl.semaphore_wait(barrier, 4 + group - 1 + cols - 1 + 2)
    tails = send_tails(pl.ds(0, 5), 0)
    loads[0].wait()
    loads[3].start()
    lax.fori_loop(0, chunks, spread, 0)
    for k in range(2):
        tail_out[starts[0] + k] = x_t[0, pad - 2 + k + seg_len]
    qtails = send_tails(pl.ds(5, 2), 2)

    def put_tails(streams):
        count = tail_in[0, 4]
        for n in streams:
            at = starts[n]
            far_last = jnp.where(s > 1, tail_in[1, at + 1], 0.0)
            far_prev = jnp.where(s > 1, tail_in[1, at], 0.0)
            last = jnp.where(count > 0.5, tail_in[0, at + 1], far_last)
            prev = jnp.where(
                count > 1.5, tail_in[0, at], jnp.where(count > 0.5, far_last, far_prev)
            )
            x_t[n, pad - 1] = jnp.where(s > 0, last, 0.0)
            x_t[n, pad - 2] = jnp.where(s > 0, prev, 0.0)

    reach = 0.5 * seg_len.astype(F32)
    middle = reach - 0.5 + shift.astype(F32)

    def featured(streams, first, stop, win):
        taps = [[taps_t[3 * n + i] for i in range(3)] for n in streams]

        def load(n, u):
            return x_t[n, pad - shift + u]

        def step(v, held):
            away, *past = held
            u = BATCH * v
            x = [
                [*before, *(load(n, u + k) for k in range(BATCH))]
                for n, before in zip(streams, past)
            ]
            kept = []
            for k in range(BATCH):
                value = None
                for w, r in zip(taps, x):
                    term = w[0] * r[k + 2] + w[1] * r[k + 1] + w[2] * r[k]
                    value = term if value is None else value * term
                kept.append(jnp.where(jnp.abs(away + float(k)) < reach, value, 0.0))
            place = pl.multiple_of(u * tiles, BATCH * tiles)
            win[pl.ds(place, BATCH * tiles), :] = jnp.concatenate(kept, axis=0).astype(BF16)
            return (away + float(BATCH), *((r[-2], r[-1]) for r in x))

        away = jnp.zeros((tiles, LANES), F32) + (first - middle)
        past = [(load(n, first - 2), load(n, first - 1)) for n in streams]
        lax.fori_loop(lax.div(first, BATCH), lax.div(stop, BATCH), step, (away, *past))

    def halo(out, into, k):
        size = half * tiles
        low, high, last = pl.ds(0, size), pl.ds(size, size), pl.ds(3 * size, size)
        return [
            remote(out.at[last], into.at[low], halo_ss.at[k], halo_rs.at[k], seq=seq_at(1)),
            remote(
                out.at[low], into.at[high], halo_ss.at[k + 1], halo_rs.at[k + 1], seq=seq_at(-1)
            ),
        ]

    halos_g = halo(g_win, g_in, 0)
    halos_f = halo(f_win, f_in, 2)

    free = rows + 8

    def front(phase, _):
        first = jnp.where(phase == 0, free, 0)
        stop = jnp.where(phase == 0, buf_rows, free)

        @pl.when(phase == 1)
        def _():
            for copy in tails:
                copy.wait_recv()
            put_tails((1, 2))

        featured((1, 2), first, stop, g_win)

        @pl.when(phase == 0)
        def _():
            halos_g[0].start()
            featured((0,), free, buf_rows, f_win)

        @pl.when(phase == 1)
        def _():
            halos_g[1].start()

        return 0

    lax.fori_loop(0, 2, front, 0)

    def wide(ref, u, count):
        place = pl.multiple_of(u * tiles, count * tiles)
        flat_rows = ref[pl.ds(place, count * tiles), :].astype(F32)
        return [flat_rows[k * tiles : (k + 1) * tiles] for k in range(count)]

    rate = rate_t[...]
    decay1 = jnp.exp(-rate)
    decays = [decay1[r] for r in range(modes)]

    def part(phase, held):
        def accumulate(v, held):
            for g in wide(g_win, BATCH * v, BATCH):
                held = [h * d + g for h, d in zip(held, decays)]
            return held

        first = jnp.where(phase == 0, 0, jnp.where(phase == 1, half, half + rows))
        stop = jnp.where(phase == 0, half, jnp.where(phase == 1, half + rows, buf_rows))
        held = lax.fori_loop(lax.div(first, BATCH), lax.div(stop, BATCH), accumulate, held)
        for r in range(modes):
            snaps[phase, r] = held[r] * decays[r]
        return held

    lax.fori_loop(0, 3, part, [jnp.zeros((tiles, LANES), F32)] * modes)
    far_out[...] = (snaps[2] * jnp.exp(float(half - rows) * rate)).reshape(flat).astype(BF16)
    far_in[0] = far_out[...]
    near_out[...] = snaps[1].reshape(flat).astype(BF16)

    def far(k):
        return remote(far_out, far_in.at[k], far_ss.at[k - 1], far_rs.at[k - 1], seq=mate(k))

    for k in range(1, group):
        far(k).start()
    near = remote(near_out, near_in, near_ss, near_rs, seq=seq_at(1))
    near.start()
    halos_f[0].start()
    for copy in qtails:
        copy.wait_recv()
    put_tails((0,))
    featured((0,), 0, free, f_win)
    halos_f[1].start()

    for copy in halos_g:
        copy.wait_recv()
    weights = [weight_t[r] for r in range(modes)]
    skip = skip_t[...]

    def joined(win, into, u):
        return [a + b for a, b in zip(wide(win, half + u, FEW), wide(into, u, FEW))]

    def tokens(v, held):
        u = FEW * v
        done = []
        for g in joined(g_win, g_in, u):
            held = [h * d + g for h, d in zip(held, decays)]
            done.append(add_all([h * w for h, w in zip(held, weights)] + [skip * g]))
        for k, value in enumerate(done):
            y_t[u + k] = value
        return held

    def local(first, stop, held):
        return lax.fori_loop(first // FEW, stop // FEW, tokens, held)

    for k in range(1, group):
        far(k).wait_send()

    def powers(blocks):
        return jnp.exp((-float(rows) * blocks.astype(F32)) * rate_t[...])

    def gather(k, _):
        source = lax.rem(pos - k + group, group)

        @pl.when(k > 0)
        def _():
            far(jnp.maximum(k, 1)).wait_recv()

        piece = far_in[k].astype(F32).reshape(shaped)
        short = piece * powers(jnp.maximum(group - 2 - source, 0))
        last = source == group - 1
        sums[0] += jnp.where(last, piece, short * powers(jnp.int32(1)))
        sums[1] += jnp.where(last, 0.0, short)
        sums[2] += jnp.where(
            (k >= 2) & (k <= pos), powers(jnp.maximum(k - 2, 0)) * piece, 0.0
        )
        return 0

    for n in range(3):
        sums[n] = jnp.zeros(shaped, F32)
    lax.fori_loop(0, group, gather, 0)
    first_down = jnp.where(pos == 0, sums[1], powers(jnp.maximum(pos - 1, 0)) * sums[0])
    col_out[0] = first_down.reshape(flat).astype(BF16)
    col_out[1] = (powers(group + pos - 1) * sums[0]).reshape(flat).astype(BF16)
    downs = [
        remote(
            col_out.at[min(k - 1, 1)],
            col_in.at[k - 1],
            col_ss.at[k - 1],
            col_rs.at[k - 1],
            seq=below(k),
        )
        for k in range(1, cols)
    ]
    for copy in downs:
        copy.start()

    local(0, rows, [jnp.zeros((tiles, LANES), F32)] * modes)

    near.wait_recv()
    carry = sums[2] + snaps[0]
    carry += jnp.where(s > 0, near_in[...].astype(F32).reshape(shaped), 0.0)
    for k, copy in enumerate(downs, 1):
        copy.wait_recv()
        piece = col_in[k - 1].astype(F32).reshape(shaped)
        if k > 2:
            piece = piece * jnp.exp(-float(rows * group * (k - 2)) * rate_t[...])
        carry += jnp.where(k <= row_id, piece, 0.0)
    carry_ref[...] = carry * weight_t[...]

    for copy in halos_f:
        copy.wait_recv()
    loads[3].wait()

    block_rows = rows // n_tp

    def mix_block(d):
        first = d * block_rows
        ahead = jnp.exp(-first.astype(F32) * rate_t[...])
        parts = [carry_ref[r] * ahead[r] for r in range(modes)]

        def mixed(v, parts):
            u = first + FEW * v
            now = [y_t[u + k] for k in range(FEW)]
            done = []
            for y, f in zip(now, joined(f_win, f_in, u)):
                done.append(f * add_all(parts + [y]))
                parts = [p * d1 for p, d1 in zip(parts, decays)]
            for k, value in enumerate(done):
                y_t[u + k] = value
            return parts

        lax.fori_loop(0, block_rows // FEW, mixed, parts)

        def lay(m, _):
            row = pl.multiple_of(first + 16 * m, 16)
            for j in range(tiles):
                mix[pl.ds(row, 16), pl.ds(j * LANES, LANES)] = y_t[pl.ds(row, 16), j, :].astype(
                    BF16
                )
            return 0

        lax.fori_loop(0, block_rows // 16, lay, 0)

    def ring(way, k, n):
        return remote(
            ring_out.at[way, k, n],
            ring_in.at[way, k + 1, n],
            ring_ss.at[way, k, n],
            ring_rs.at[way, k, n],
            tp=tp_at(1 - 2 * way),
        )

    def pieces(t, _):
        way = lax.rem(t, 2)
        n = lax.rem(lax.div(t, 2), SUB)
        k = lax.div(t, 2 * SUB)
        block = lax.rem(me - (1 - 2 * way) * (k + 1) + 2 * n_tp, n_tp)

        @pl.when((t == 0) | (t == 1) | (t == 2 * SUB) | (t == 6 * SUB))
        def _():
            mix_block(block)

        col = pl.multiple_of((way * SUB + n) * piece_cols, piece_cols)
        total = jnp.dot(
            mix[pl.ds(pl.multiple_of(block * block_rows, block_rows), block_rows), :],
            w_ref[:, pl.ds(col, piece_cols)],
            preferred_element_type=F32,
        )

        @pl.when(k > 0)
        def _():
            ring(way, jnp.maximum(k - 1, 0), n).wait_recv()

        total = (total + ring_in[way, k, n].astype(F32)).astype(BF16)

        @pl.when(k < n_tp - 1)
        def _():
            safe = jnp.minimum(k, n_tp - 2)
            ring_out[way, safe, n] = total

            @pl.when(k * SUB + n >= FLIGHT)
            def _():
                past = jnp.maximum(k * SUB + n - FLIGHT, 0)
                ring(way, lax.div(past, SUB), lax.rem(past, SUB)).wait_send()

            ring(way, safe, n).start()

        @pl.when(k == n_tp - 1)
        def _():
            out_ref[:, pl.ds(col, piece_cols)] = total

        return 0

    lax.fori_loop(0, 2 * SUB * n_tp, pieces, 0)

    for copy in tails + qtails + halos_g + halos_f + [near] + downs:
        copy.wait_send()

    def drain(t, _):
        ring(lax.rem(t, 2), lax.div(t, 2 * SUB), lax.rem(lax.div(t, 2), SUB)).wait_send()
        return 0

    lax.fori_loop(2 * (SUB * (n_tp - 1) - FLIGHT), 2 * SUB * (n_tp - 1), drain, 0)


def shards(
    n_seq, n_tp, tokens, seg_length, seg_offset, short_weight, residues, spans, skip_gain, out_weight
):
    buf_rows, _, chans = tokens.shape
    rows = buf_rows // 2
    modes = residues.shape[0]
    tiles = chans // LANES
    group = min(ROW_GROUP, n_seq)
    cols = n_seq // group
    out_cols = out_weight.shape[1]
    block_rows = rows // n_tp
    vmem = pl.BlockSpec(memory_space=pltpu.VMEM)
    smem = pl.BlockSpec(memory_space=pltpu.SMEM)
    hbm = pl.BlockSpec(memory_space=pl.ANY)
    piece = (SUB, block_rows, out_cols // (2 * SUB))
    dma = pltpu.SemaphoreType.DMA
    state = (modes, tiles, LANES)
    flat = (modes * tiles, LANES)
    return pl.pallas_call(
        functools.partial(kernel, n_seq, n_tp),
        out_shape=jax.ShapeDtypeStruct((block_rows, out_cols), BF16),
        in_specs=[smem, smem, hbm, vmem, vmem, vmem, vmem, hbm],
        out_specs=vmem,
        scratch_shapes=[
            pltpu.VMEM((3, buf_rows, chans), BF16),
            pltpu.VMEM((chans, out_cols), BF16),
            pltpu.VMEM((3, rows + HEAD + buf_rows, tiles, LANES), F32),
            pltpu.VMEM((9, tiles, LANES), F32),
            pltpu.VMEM((7, tiles, LANES), F32),
            pltpu.VMEM((2, 7, tiles, LANES), F32),
            pltpu.VMEM((buf_rows * tiles, LANES), BF16),
            pltpu.VMEM((rows * tiles, LANES), BF16),
            pltpu.VMEM((buf_rows * tiles, LANES), BF16),
            pltpu.VMEM((rows * tiles, LANES), BF16),
            pltpu.VMEM((3, *state), F32),
            pltpu.VMEM(flat, BF16),
            pltpu.VMEM(flat, BF16),
            pltpu.VMEM(flat, BF16),
            pltpu.VMEM((group, *flat), BF16),
            pltpu.VMEM((3, *state), F32),
            pltpu.VMEM((2, *flat), BF16),
            pltpu.VMEM((cols - 1, *flat), BF16),
            pltpu.VMEM(state, F32),
            pltpu.VMEM(state, F32),
            pltpu.VMEM(state, F32),
            pltpu.VMEM((tiles, LANES), F32),
            pltpu.VMEM((rows, tiles, LANES), F32),
            pltpu.VMEM((rows, chans), BF16),
            pltpu.VMEM((2, n_tp - 1, *piece), BF16),
            pltpu.VMEM((2, n_tp, *piece), BF16),
            dma((4,)),
            dma((4,)),
            dma((4,)),
            dma((4,)),
            dma((4,)),
            dma,
            dma,
            dma((group - 1,)),
            dma((group - 1,)),
            dma((cols - 1,)),
            dma((cols - 1,)),
            dma((2, n_tp - 1, SUB)),
            dma((2, n_tp - 1, SUB)),
        ],
        compiler_params=pltpu.CompilerParams(
            collective_id=0, has_side_effects=True, vmem_limit_bytes=60 * 1024 * 1024
        ),
        name="hyena_mixer",
    )(
        seg_length,
        seg_offset,
        jnp.transpose(tokens, (1, 0, 2)),
        short_weight,
        residues,
        spans,
        skip_gain[None, :],
        out_weight,
    )


def solution(mesh):
    in_specs = (
        P("seq", None, "tp"),
        P("seq"),
        P("seq"),
        P(None, None, "tp"),
        P(None, "tp"),
        P(None, "tp"),
        P("tp"),
        P("tp", None),
    )
    out_specs = P(("seq", "tp"), None)
    body = functools.partial(shards, mesh.shape["seq"], mesh.shape["tp"])
    return jax.shard_map(body, mesh=mesh, in_specs=in_specs, out_specs=out_specs, check_vma=False)
```

time: 82.6 us -> 78.3 us (0.948)
  Pallas kernels: 78.8 us -> 74.5 us
    pallas_call x1, Pallas kernels: 78.8 us -> 74.5 us  [shards(): pl.pallas_call(functools.partial(kernel, n_seq, n_tp), out_shape=jax.Shap...]
where the time goes in v3:
time: 78.3 us; the launch traced here: 78.1 us
  Pallas kernels  74.5 us (95%)
  local copies, waits for them, and re-layouts  2.29 us (3%)
  between operations  1.3 us (2%)
    pallas_call x1, Pallas kernels, shards(): pl.pallas_call(functools.partial(kernel, n_seq, n_tp), out_shape=jax.Shap...  74.5 us
    unnamed x1, local copies, waits for them, and re-layouts  2.29 us

profile of v3, /device:TPU:1, one launch (start us, length us, event | category | flops | bytes accessed | tf_op | source)
XLA Modules:
  0.0 78.1 jit_solution(8958266061294358415)
XLA Ops:
  1.3 74.5 %hyena_mixer.1 = bf16[128,4096]{1,0:T(8,128)(2,1)} custom-call(s32[1]{0:T(128)S(6)} %copy.10.len_ref, s32[1]{0:T(128)S(6)} %copy.11.off_ref, bf16[3,1024,1024]{2,1,0:T(8,128)(2,1)} %bitcast.2, f32[3,3,1024]{2,1,0:T(4,128)} %taps_ref.1, f32[16,1024]{1,0:T(8,128)} %res_ref.1, f32[16,1024]{1,0:T(8,128)} %span_ref.1, f32[1,1024]{1,0:T(1,128)} %bitcast.3, ...), custom_call_target="tpu_custom_call" | custom-call | tf_op jit(solution)/shard_map/hyena_mixer/pallas_call | solution.py:527
  75.8 2.3 %copy.12 = bf16[128,4096]{1,0:T(8,128)(2,1)} copy(bf16[128,4096]{1,0:T(8,128)(2,1)} %hyena_mixer.1) | data formatting | bytes 2097152

commit v4 on v3

--- a/solution.py
+++ b/solution.py
@@ -142,11 +142,11 @@
     seg_len = jnp.clip(len_ref[0], 0, buf_rows)
     shift = jnp.clip(off_ref[0] - (rows * s - half), 0, rows)
 
+    rate = 1.0 / span_ref[...]
+    rate_t[...] = rate.reshape(shaped)
+    weight_t[...] = (res_ref[...] * jnp.sqrt(rate)).reshape(shaped)
     for j in range(tiles):
         lane = pl.ds(j * LANES, LANES)
-        rate = 1.0 / span_ref[:, lane]
-        rate_t[:, j, :] = rate
-        weight_t[:, j, :] = res_ref[:, lane] * jnp.sqrt(rate)
         skip_t[pl.ds(j, 1), :] = skip_ref[:, lane]
         for i in range(3):
             for n in range(3):
@@ -436,10 +436,7 @@
 
         def lay(m, _):
             row = pl.multiple_of(first + 16 * m, 16)
-            for j in range(tiles):
-                mix[pl.ds(row, 16), pl.ds(j * LANES, LANES)] = y_t[pl.ds(row, 16), j, :].astype(
-                    BF16
-                )
+            mix[pl.ds(row, 16), :] = y_t[pl.ds(row, 16)].reshape(16, chans).astype(BF16)
             return 0
 
         lax.fori_loop(0, block_rows // 16, lay, 0)

time: 78.3 us -> 77.9 us (level)
  no operation moved by 1% of the time
where the time goes in v4:
time: 77.9 us; the launch traced here: 77.7 us
  Pallas kernels  74.1 us (95%)
  local copies, waits for them, and re-layouts  2.29 us (3%)
  between operations  1.3 us (2%)
    pallas_call x1, Pallas kernels, shards(): pl.pallas_call(functools.partial(kernel, n_seq, n_tp), out_shape=jax.Shap...  74.1 us
    unnamed x1, local copies, waits for them, and re-layouts  2.29 us

profile of v4, /device:TPU:1, one launch (start us, length us, event | category | flops | bytes accessed | tf_op | source)
XLA Modules:
  0.0 77.7 jit_solution(4918109929082487590)
XLA Ops:
  1.3 74.1 %hyena_mixer.1 = bf16[128,4096]{1,0:T(8,128)(2,1)} custom-call(s32[1]{0:T(128)S(6)} %copy.10.len_ref, s32[1]{0:T(128)S(6)} %copy.11.off_ref, bf16[3,1024,1024]{2,1,0:T(8,128)(2,1)} %bitcast.2, f32[3,3,1024]{2,1,0:T(4,128)} %taps_ref.1, f32[16,1024]{1,0:T(8,128)} %res_ref.1, f32[16,1024]{1,0:T(8,128)} %span_ref.1, f32[1,1024]{1,0:T(1,128)} %bitcast.3, ...), custom_call_target="tpu_custom_call" | custom-call | tf_op jit(solution)/shard_map/hyena_mixer/pallas_call | solution.py:524
  75.4 2.3 %copy.12 = bf16[128,4096]{1,0:T(8,128)(2,1)} copy(bf16[128,4096]{1,0:T(8,128)(2,1)} %hyena_mixer.1) | data formatting | bytes 2097152
